TPU v7x, 32 devices: a whole 2x2x4 slice. The times are simulated.
32 devices in a mesh: dp: 2 (over y), ctx: 16 (over z, x, core).
Axes of the slice: x: 2, y: 2, z: 4, core: 2. Of those that a mesh axis runs over, the one named last changes fastest.
Arguments:
- receptance: bfloat16 [4096, 512], P(('dp', 'ctx')), parts along dimension 0, may hold values from -0.75 to 0.75
- token_key: bfloat16 [4096, 512], P(('dp', 'ctx')), parts along dimension 0, may hold values from -0.75 to 0.75
- token_value: bfloat16 [4096, 512], P(('dp', 'ctx')), parts along dimension 0, may hold values from -0.75 to 0.75
- kappa_raw: bfloat16 [4096, 512], P(('dp', 'ctx')), parts along dimension 0, may hold values from -6 to 6
- removal: bfloat16 [4096, 512], P(('dp', 'ctx')), parts along dimension 0, may hold values from 0.0099487305 to 0.029907227
- decay_rate: float32 [4096, 512], P(('dp', 'ctx')), parts along dimension 0, may hold values from 0 to 1
- shard_length: int32 [32], P(('dp', 'ctx')), parts along dimension 0, may hold values from 32 to 128, as said below
- grad_output: bfloat16 [4096, 512], P(('dp', 'ctx')), parts along dimension 0, may hold values from -0.75 to 0.75
Outputs:
- mixed_out: bfloat16 [4096, 512], P(('dp', 'ctx')), parts along dimension 0
- grad_receptance: bfloat16 [4096, 512], P(('dp', 'ctx')), parts along dimension 0
- grad_key: bfloat16 [4096, 512], P(('dp', 'ctx')), parts along dimension 0
- grad_value: bfloat16 [4096, 512], P(('dp', 'ctx')), parts along dimension 0
There are 2 independent parts, one for each index of `dp`. A program takes and returns all parts, laid end to end along the dimension named above; each array names one. Nothing has to cross between parts.
Inputs may be any that keep to these rules, and one draw needn't show every extreme that they name: `shard_length`: in every draw some shard has all 128 tokens live.
All inputs are finite; a program needn't handle non-finite values.
Results may differ from a plain program's by a relative error of at most 0.0017.
The roundings to bfloat16 on the way count: a program that leaves them out, or rounds other values in their place, can miss the bound.
Values sent between devices are 32-bit elements; how exact they have to be, the bound alone decides.
A program may use at most 192 MiB of HBM per device.

v0:
```python
import jax
import jax.numpy as jnp
from jax import lax
from jax.sharding import PartitionSpec as P

H = 8
HS = 64


HIGHEST = lax.Precision.HIGHEST


def carried_in(part, axis, combine, identity, reverse):
    count = lax.axis_size(axis)
    place = lax.axis_index(axis)
    ahead = count - 1 - place if reverse else place
    gathered = jax.tree.map(lambda a: lax.all_gather(a, axis), part)
    state = jax.tree.map(lambda a, e: jnp.zeros_like(a) + jnp.asarray(e, a.dtype), part, identity)

    def one(step, state):
        source = count - 1 - step if reverse else step
        return combine(
            state, jax.tree.map(lambda a: lax.dynamic_index_in_dim(a, source, 0, False), gathered)
        )

    return lax.fori_loop(0, ahead, one, state)


def advance(state, decays, unit_kappa, erase_dir):
    along = jnp.einsum("hvk,hk->hv", state, unit_kappa, precision=HIGHEST)
    return state * decays[:, None, :] - along[:, :, None] * erase_dir[:, None, :]


def retreat(adjoint, decays, unit_kappa, erase_dir):
    along = jnp.einsum("hvk,hk->hv", adjoint, erase_dir, precision=HIGHEST)
    return adjoint * decays[:, None, :] - along[:, :, None] * unit_kappa[:, None, :]


def rank_one(left, right):
    return left[:, :, None] * right[:, None, :]


def compose(earlier, later):
    first_map, first_shift = earlier
    second_map, second_shift = later
    joined = jnp.einsum("hij,hjk->hik", first_map, second_map, precision=HIGHEST)
    moved = jnp.einsum("hvj,hjk->hvk", first_shift, second_map, precision=HIGHEST) + second_shift
    return (joined, moved)


def local(
    receptance, token_key, token_value, kappa_raw, removal, decay_rate, shard_length, grad_output
):
    tokens = receptance.shape[0]
    heads = H
    width = HS
    span = 32
    blocks = tokens // span
    position = lax.broadcasted_iota(jnp.int32, (tokens, 1), 0)
    live = (position < shard_length[0]).astype(jnp.float32)

    def split(values):
        return values.reshape(tokens, heads, width)

    decays = split(jnp.exp(-decay_rate * live))
    kappa = split(kappa_raw.astype(jnp.float32))
    unit_kappa = kappa / jnp.sqrt(jnp.sum(kappa * kappa, axis=-1, keepdims=True) + 1e-05)
    erase_dir = split(removal.astype(jnp.float32) * live) * unit_kappa
    read_vec = split(receptance.astype(jnp.float32) * live)
    key_vec = split(token_key.astype(jnp.float32) * live)
    value_vec = split(token_value.astype(jnp.float32) * live)
    grad_vec = split(grad_output.astype(jnp.float32) * live)
    series = tuple(
        (
            member.reshape(blocks, span, heads, width)
            for member in (decays, unit_kappa, erase_dir, read_vec, key_vec, value_vec, grad_vec)
        )
    )
    identity = jnp.broadcast_to(jnp.eye(width, dtype=jnp.float32), (heads, width, width))
    blank = jnp.zeros((heads, width, width), jnp.float32)

    def forward_totals(both, block):
        for within in range(span):
            doubled = [
                jnp.concatenate([block[member][within], block[member][within]], axis=0)
                for member in range(3)
            ]
            fresh = jnp.concatenate([blank, rank_one(block[5][within], block[4][within])], axis=0)
            both = advance(both, doubled[0], doubled[1], doubled[2]) + fresh
        return (both, None)

    def backward_totals(carry, block):
        for within in reversed(range(span)):
            adjoint = carry + rank_one(block[6][within], block[3][within])
            carry = retreat(adjoint, block[0][within], block[1][within], block[2][within])
        return (carry, None)

    both, unused = lax.scan(forward_totals, jnp.concatenate([identity, blank], axis=0), series)
    product = both[:heads]
    accumulated = both[heads:]
    carry_back, unused = lax.scan(backward_totals, blank, series, reverse=True)
    transposed = jnp.swapaxes(product, 1, 2)
    incoming = carried_in((product, accumulated), "ctx", compose, (identity, blank), False)[1]
    from_later = carried_in((transposed, carry_back), "ctx", compose, (identity, blank), True)[1]

    def forward_exact(state, block):
        states = []
        for within in range(span):
            state = advance(state, block[0][within], block[1][within], block[2][within]) + rank_one(
                block[5][within], block[4][within]
            )
            states.append(state.astype(jnp.bfloat16))
        stacked = jnp.stack(states)
        outputs = jnp.einsum(
            "thvk,thk->thv",
            stacked,
            block[3].astype(jnp.bfloat16),
            preferred_element_type=jnp.float32,
        )
        grads = jnp.einsum(
            "thvk,thv->thk",
            stacked,
            block[6].astype(jnp.bfloat16),
            preferred_element_type=jnp.float32,
        )
        return (state, (outputs, grads))

    def backward_exact(carry, block):
        adjoints = [None] * span
        for within in reversed(range(span)):
            adjoint = carry + rank_one(block[6][within], block[3][within])
            adjoints[within] = adjoint.astype(jnp.bfloat16)
            carry = retreat(adjoint, block[0][within], block[1][within], block[2][within])
        stacked = jnp.stack(adjoints)
        value_grads = jnp.einsum(
            "thvk,thk->thv",
            stacked,
            block[4].astype(jnp.bfloat16),
            preferred_element_type=jnp.float32,
        )
        key_grads = jnp.einsum(
            "thvk,thv->thk",
            stacked,
            block[5].astype(jnp.bfloat16),
            preferred_element_type=jnp.float32,
        )
        return (carry, (value_grads, key_grads))

    unused, (mixed, grad_read) = lax.scan(forward_exact, incoming, series)
    unused, (grad_val, grad_keys) = lax.scan(backward_exact, from_later, series, reverse=True)
    channels = heads * width
    return (
        mixed.reshape(tokens, channels).astype(jnp.bfloat16),
        grad_read.reshape(tokens, channels).astype(jnp.bfloat16),
        grad_keys.reshape(tokens, channels).astype(jnp.bfloat16),
        grad_val.reshape(tokens, channels).astype(jnp.bfloat16),
    )


def solution(mesh):
    placed = (
        P(("dp", "ctx"), None),
        P(("dp", "ctx"), None),
        P(("dp", "ctx"), None),
        P(("dp", "ctx"), None),
        P(("dp", "ctx"), None),
        P(("dp", "ctx"), None),
        P(("dp", "ctx")),
        P(("dp", "ctx"), None),
    )
    return jax.shard_map(
        local,
        mesh=mesh,
        in_specs=placed,
        out_specs=(
            P(("dp", "ctx"), None),
            P(("dp", "ctx"), None),
            P(("dp", "ctx"), None),
            P(("dp", "ctx"), None),
        ),
        check_vma=False,
    )
```

profile of v0, /device:TPU:1, one launch (start us, length us, event | category | flops | bytes accessed | tf_op | source)
XLA Modules:
  0.0 1524.1 jit_solution(18433635573530281979)
XLA Ops:
  15.3 175.5 %while.83 = (s32[]{:T(128)}, f32[16,64,64]{2,1,0:T(8,128)S(1)}, f32[4,32,8,64]{3,2,1,0:T(8,128)S(1)}, f32[4,32,8,64]{3,2,1,0:T(8,128)S(1)}, f32[4,32,8,64]{3,2,1...) while((s32[]{:T(128)}, f32[16,64,64]{2,1,0:T(8,128)S(1)}, ...), condition=%wide.region_2.3_spmd, body=%wide.region_1.2_spmd.sunk | while | flops 38895648 | bytes 29656860 | solution.py:98
  196.3 344.0 %while.88 = (s32[]{:T(128)}, f32[8,64,64]{2,1,0:T(8,128)S(1)}, f32[4,32,8,64]{3,2,1,0:T(8,128)}, f32[4,32,8,64]{3,2,1,0:T(8,128)S(1)}, f32[4,32,8,64]{3,2,1,0:T(...) while((s32[]{:T(128)}, f32[8,64,64]{2,1,0:T(8,128)S(1)}, ...), condition=%wide.region_8.9_spmd.clone, body=%wide.region_7.8_spmd.clone.sunk | while | flops 44072992 | bytes 9715269 | solution.py:101
  276.7 5.7 multiply_add_fusion.375
  286.4 6.6 multiply_subtract_fusion.5
  351.8 5.7 multiply_add_fusion.375
  361.6 6.6 multiply_subtract_fusion.5
  426.9 5.7 multiply_add_fusion.375
  436.7 6.6 multiply_subtract_fusion.5
  502.0 5.7 multiply_add_fusion.375
  511.8 6.6 multiply_subtract_fusion.5
  548.8 266.2 %while.85 = (s32[]{:T(128)}, f32[8,64,64]{2,1,0:T(8,128)S(1)}, bf16[4,32,8,64]{3,2,1,0:T(8,128)(2,1)S(1)}, bf16[4,32,8,64]{3,2,1,0:T(8,128)(2,1)}, f32[4,32,8,64...) while((s32[]{:T(128)}, f32[8,64,64]{2,1,0:T(8,128)S(1)}, ...), condition=%wide.region_6.7_spmd, body=%wide.region_5.6_spmd.sunk | while | flops 38797344 | bytes 30213484 | solution.py:149
  817.7 38.1 %while.86 = (s32[]{:T(128)}, f32[8,64,64]{1,2,0:T(8,128)S(1)}, s32[]{:T(128)}, f32[16,8,64,64]{3,2,1,0:T(8,128)}, f32[16,8,64,64]{3,2,1,0:T(8,128)}, /*index=5*/s32[]{:T(128)}, s32[]{:T(128)}, s32[]{:T(128)}, s32[]{:T(128)}) while((s32[]{:T(128)}, f32[8,64,64]{1,2,0:T(8,128)S(1)}, s32[]{:T(128)}, f32[16,8,64,64]{3,2,1,0:T(8,128)}, ...), condition=%wide.region_10.11_spmd, body=%wide.region_9.10_spmd.sunk | while | flops 25198596 | bytes 1441947 | solution.py:26
  856.0 659.4 %while.87 = (s32[]{:T(128)}, f32[8,64,64]{2,1,0:T(8,128)S(1)}, bf16[4,32,8,64]{3,2,1,0:T(8,128)(2,1)S(1)}, bf16[4,32,8,64]{3,2,1,0:T(8,128)(2,1)S(1)}, f32[4,32,...) while((s32[]{:T(128)}, f32[8,64,64]{2,1,0:T(8,128)S(1)}, ...), condition=%wide.region_12.13_spmd, body=%wide.region_11.12_spmd.sunk | while | flops 132317216 | bytes 36621612 | solution.py:150
  900.4 5.6 multiply_add_fusion.344
  909.0 6.2 bitcast_dynamic-update-slice_fusion.158
  915.2 6.2 bitcast_dynamic-update-slice_fusion.159
  921.4 6.0 bitcast_dynamic-update-slice_fusion.160
  927.4 5.8 bitcast_dynamic-update-slice_fusion.161
  933.2 5.6 bitcast_dynamic-update-slice_fusion.162
  938.7 5.4 bitcast_dynamic-update-slice_fusion.163
  949.3 5.4 bitcast_dynamic-update-slice_fusion.165
  1012.4 6.6 multiply_subtract_fusion.4
  1063.9 5.6 multiply_add_fusion.344
  1072.4 6.3 bitcast_dynamic-update-slice_fusion.158
  1078.7 6.2 bitcast_dynamic-update-slice_fusion.159
  1084.9 6.0 bitcast_dynamic-update-slice_fusion.160
  1090.9 5.8 bitcast_dynamic-update-slice_fusion.161
  1096.7 5.6 bitcast_dynamic-update-slice_fusion.162
  1112.8 5.4 bitcast_dynamic-update-slice_fusion.165
  1176.0 6.6 multiply_subtract_fusion.4
  1227.4 5.6 multiply_add_fusion.344
  1236.0 6.3 bitcast_dynamic-update-slice_fusion.158
  1242.3 6.2 bitcast_dynamic-update-slice_fusion.159
  1248.4 6.0 bitcast_dynamic-update-slice_fusion.160
  1254.4 5.8 bitcast_dynamic-update-slice_fusion.161
  1260.2 5.6 bitcast_dynamic-update-slice_fusion.162
  1265.8 5.4 bitcast_dynamic-update-slice_fusion.163
  1276.3 5.4 bitcast_dynamic-update-slice_fusion.165
  1339.6 6.6 multiply_subtract_fusion.4
  1391.0 5.6 multiply_add_fusion.344
  1399.6 6.3 bitcast_dynamic-update-slice_fusion.158
  1405.8 6.2 bitcast_dynamic-update-slice_fusion.159
  1412.0 6.0 bitcast_dynamic-update-slice_fusion.160
  1418.0 5.8 bitcast_dynamic-update-slice_fusion.161
  1423.8 5.6 bitcast_dynamic-update-slice_fusion.162
  1429.4 5.4 bitcast_dynamic-update-slice_fusion.163
  1439.9 5.4 bitcast_dynamic-update-slice_fusion.165
  1503.1 6.6 multiply_subtract_fusion.4
  (2331 shorter events, 1196.1 us)
Async XLA Ops:
  7.2 537.9 %all-gather.9.cloned.1.call-start = ((), (), s32[]{:S(2)}) async-start(), calls=%async_computation | async-start | bytes 4456448 | tf_op jit(solution)/shard_map/all_gather | solution.py:17
  191.6 353.5 %all-gather.11.cloned.1.call-start = ((), (), s32[]{:S(2)}) async-start(), calls=%async_computation.1 | async-start | bytes 4456448 | tf_op jit(solution)/shard_map/all_gather | solution.py:17
  192.4 625.3 %all-gather.13.cloned.1.call-start = ((), (), s32[]{:S(2)}) async-start(), calls=%async_computation.2 | async-start | bytes 4456448 | tf_op jit(solution)/shard_map/all_gather | solution.py:17
  193.3 624.4 %all-gather.15.cloned.1.call-start = ((), (), s32[]{:S(2)}) async-start(), calls=%async_computation.3 | async-start | bytes 4456448 | tf_op jit(solution)/shard_map/all_gather | solution.py:17
  247.9 25.0 %copy-start.56 = (f32[8,64]{1,0:T(8,128)S(1)}, f32[8,64]{1,0:T(8,128)}, u32[]{:S(2)}) copy-start(f32[8,64]{1,0:T(8,128)} %get-tuple-element.3449) | copy-start | bytes 6148 | tf_op jit(solution)/shard_map/while
  247.9 25.0 %copy-start.60 = (f32[8,64]{1,0:T(8,128)S(1)}, f32[8,64]{1,0:T(8,128)}, u32[]{:S(2)}) copy-start(f32[8,64]{1,0:T(8,128)} %get-tuple-element.3447) | copy-start | bytes 6148 | tf_op jit(solution)/shard_map/while
  247.9 25.0 %copy-start.64 = (f32[8,64]{1,0:T(8,128)S(1)}, f32[8,64]{1,0:T(8,128)}, u32[]{:S(2)}) copy-start(f32[8,64]{1,0:T(8,128)} %get-tuple-element.3448) | copy-start | bytes 6148 | tf_op jit(solution)/shard_map/while
  248.0 26.2 %copy-start.55 = (f32[8,64]{1,0:T(8,128)S(1)}, f32[8,64]{1,0:T(8,128)}, u32[]{:S(2)}) copy-start(f32[8,64]{1,0:T(8,128)} %get-tuple-element.3445) | copy-start | bytes 6148 | tf_op jit(solution)/shard_map/while
  248.0 26.1 %copy-start.59 = (f32[8,64]{1,0:T(8,128)S(1)}, f32[8,64]{1,0:T(8,128)}, u32[]{:S(2)}) copy-start(f32[8,64]{1,0:T(8,128)} %get-tuple-element.3443) | copy-start | bytes 6148 | tf_op jit(solution)/shard_map/while
  248.0 26.1 %copy-start.63 = (f32[8,64]{1,0:T(8,128)S(1)}, f32[8,64]{1,0:T(8,128)}, u32[]{:S(2)}) copy-start(f32[8,64]{1,0:T(8,128)} %get-tuple-element.3444) | copy-start | bytes 6148 | tf_op jit(solution)/shard_map/while
  256.9 25.9 %copy-start.65 = (f32[8,64]{1,0:T(8,128)S(1)}, f32[8,64]{1,0:T(8,128)}, u32[]{:S(2)}) copy-start(f32[8,64]{1,0:T(8,128)} %get-tuple-element.3461) | copy-start | bytes 6148 | tf_op jit(solution)/shard_map/while
  256.9 25.9 %copy-start.70 = (f32[8,64]{1,0:T(8,128)S(1)}, f32[8,64]{1,0:T(8,128)}, u32[]{:S(2)}) copy-start(f32[8,64]{1,0:T(8,128)} %get-tuple-element.3459) | copy-start | bytes 6148 | tf_op jit(solution)/shard_map/while
  257.0 25.9 %copy-start.74 = (f32[8,64]{1,0:T(8,128)S(1)}, f32[8,64]{1,0:T(8,128)}, u32[]{:S(2)}) copy-start(f32[8,64]{1,0:T(8,128)} %get-tuple-element.3460) | copy-start | bytes 6148 | tf_op jit(solution)/shard_map/while
  257.0 26.6 %copy-start.68 = (f32[8,64]{1,0:T(8,128)S(1)}, f32[8,64]{1,0:T(8,128)}, u32[]{:S(2)}) copy-start(f32[8,64]{1,0:T(8,128)} %get-tuple-element.3457) | copy-start | bytes 6148 | tf_op jit(solution)/shard_map/while
  257.0 26.6 %copy-start.72 = (f32[8,64]{1,0:T(8,128)S(1)}, f32[8,64]{1,0:T(8,128)}, u32[]{:S(2)}) copy-start(f32[8,64]{1,0:T(8,128)} %get-tuple-element.3455) | copy-start | bytes 6148 | tf_op jit(solution)/shard_map/while
  257.0 26.6 %copy-start.76 = (f32[8,64]{1,0:T(8,128)S(1)}, f32[8,64]{1,0:T(8,128)}, u32[]{:S(2)}) copy-start(f32[8,64]{1,0:T(8,128)} %get-tuple-element.3456) | copy-start | bytes 6148 | tf_op jit(solution)/shard_map/while
  323.0 25.0 %copy-start.64 = (f32[8,64]{1,0:T(8,128)S(1)}, f32[8,64]{1,0:T(8,128)}, u32[]{:S(2)}) copy-start(f32[8,64]{1,0:T(8,128)} %get-tuple-element.3448) | copy-start | bytes 6148 | tf_op jit(solution)/shard_map/while
  323.1 26.2 %copy-start.55 = (f32[8,64]{1,0:T(8,128)S(1)}, f32[8,64]{1,0:T(8,128)}, u32[]{:S(2)}) copy-start(f32[8,64]{1,0:T(8,128)} %get-tuple-element.3445) | copy-start | bytes 6148 | tf_op jit(solution)/shard_map/while
  323.1 26.1 %copy-start.59 = (f32[8,64]{1,0:T(8,128)S(1)}, f32[8,64]{1,0:T(8,128)}, u32[]{:S(2)}) copy-start(f32[8,64]{1,0:T(8,128)} %get-tuple-element.3443) | copy-start | bytes 6148 | tf_op jit(solution)/shard_map/while
  323.2 26.2 %copy-start.63 = (f32[8,64]{1,0:T(8,128)S(1)}, f32[8,64]{1,0:T(8,128)}, u32[]{:S(2)}) copy-start(f32[8,64]{1,0:T(8,128)} %get-tuple-element.3444) | copy-start | bytes 6148 | tf_op jit(solution)/shard_map/while
  332.1 25.9 %copy-start.65 = (f32[8,64]{1,0:T(8,128)S(1)}, f32[8,64]{1,0:T(8,128)}, u32[]{:S(2)}) copy-start(f32[8,64]{1,0:T(8,128)} %get-tuple-element.3461) | copy-start | bytes 6148 | tf_op jit(solution)/shard_map/while
  332.1 25.9 %copy-start.70 = (f32[8,64]{1,0:T(8,128)S(1)}, f32[8,64]{1,0:T(8,128)}, u32[]{:S(2)}) copy-start(f32[8,64]{1,0:T(8,128)} %get-tuple-element.3459) | copy-start | bytes 6148 | tf_op jit(solution)/shard_map/while
  332.1 25.9 %copy-start.74 = (f32[8,64]{1,0:T(8,128)S(1)}, f32[8,64]{1,0:T(8,128)}, u32[]{:S(2)}) copy-start(f32[8,64]{1,0:T(8,128)} %get-tuple-element.3460) | copy-start | bytes 6148 | tf_op jit(solution)/shard_map/while
  332.1 26.6 %copy-start.68 = (f32[8,64]{1,0:T(8,128)S(1)}, f32[8,64]{1,0:T(8,128)}, u32[]{:S(2)}) copy-start(f32[8,64]{1,0:T(8,128)} %get-tuple-element.3457) | copy-start | bytes 6148 | tf_op jit(solution)/shard_map/while
  332.1 26.6 %copy-start.72 = (f32[8,64]{1,0:T(8,128)S(1)}, f32[8,64]{1,0:T(8,128)}, u32[]{:S(2)}) copy-start(f32[8,64]{1,0:T(8,128)} %get-tuple-element.3455) | copy-start | bytes 6148 | tf_op jit(solution)/shard_map/while
  332.1 26.6 %copy-start.76 = (f32[8,64]{1,0:T(8,128)S(1)}, f32[8,64]{1,0:T(8,128)}, u32[]{:S(2)}) copy-start(f32[8,64]{1,0:T(8,128)} %get-tuple-element.3456) | copy-start | bytes 6148 | tf_op jit(solution)/shard_map/while
  398.1 25.0 %copy-start.60 = (f32[8,64]{1,0:T(8,128)S(1)}, f32[8,64]{1,0:T(8,128)}, u32[]{:S(2)}) copy-start(f32[8,64]{1,0:T(8,128)} %get-tuple-element.3447) | copy-start | bytes 6148 | tf_op jit(solution)/shard_map/while
  398.1 25.0 %copy-start.64 = (f32[8,64]{1,0:T(8,128)S(1)}, f32[8,64]{1,0:T(8,128)}, u32[]{:S(2)}) copy-start(f32[8,64]{1,0:T(8,128)} %get-tuple-element.3448) | copy-start | bytes 6148 | tf_op jit(solution)/shard_map/while
  398.3 26.2 %copy-start.55 = (f32[8,64]{1,0:T(8,128)S(1)}, f32[8,64]{1,0:T(8,128)}, u32[]{:S(2)}) copy-start(f32[8,64]{1,0:T(8,128)} %get-tuple-element.3445) | copy-start | bytes 6148 | tf_op jit(solution)/shard_map/while
  398.3 26.1 %copy-start.59 = (f32[8,64]{1,0:T(8,128)S(1)}, f32[8,64]{1,0:T(8,128)}, u32[]{:S(2)}) copy-start(f32[8,64]{1,0:T(8,128)} %get-tuple-element.3443) | copy-start | bytes 6148 | tf_op jit(solution)/shard_map/while
  398.3 26.1 %copy-start.63 = (f32[8,64]{1,0:T(8,128)S(1)}, f32[8,64]{1,0:T(8,128)}, u32[]{:S(2)}) copy-start(f32[8,64]{1,0:T(8,128)} %get-tuple-element.3444) | copy-start | bytes 6148 | tf_op jit(solution)/shard_map/while
  407.2 25.9 %copy-start.65 = (f32[8,64]{1,0:T(8,128)S(1)}, f32[8,64]{1,0:T(8,128)}, u32[]{:S(2)}) copy-start(f32[8,64]{1,0:T(8,128)} %get-tuple-element.3461) | copy-start | bytes 6148 | tf_op jit(solution)/shard_map/while
  407.2 25.9 %copy-start.70 = (f32[8,64]{1,0:T(8,128)S(1)}, f32[8,64]{1,0:T(8,128)}, u32[]{:S(2)}) copy-start(f32[8,64]{1,0:T(8,128)} %get-tuple-element.3459) | copy-start | bytes 6148 | tf_op jit(solution)/shard_map/while
  407.2 25.9 %copy-start.74 = (f32[8,64]{1,0:T(8,128)S(1)}, f32[8,64]{1,0:T(8,128)}, u32[]{:S(2)}) copy-start(f32[8,64]{1,0:T(8,128)} %get-tuple-element.3460) | copy-start | bytes 6148 | tf_op jit(solution)/shard_map/while
  407.2 26.6 %copy-start.68 = (f32[8,64]{1,0:T(8,128)S(1)}, f32[8,64]{1,0:T(8,128)}, u32[]{:S(2)}) copy-start(f32[8,64]{1,0:T(8,128)} %get-tuple-element.3457) | copy-start | bytes 6148 | tf_op jit(solution)/shard_map/while
  407.2 26.6 %copy-start.72 = (f32[8,64]{1,0:T(8,128)S(1)}, f32[8,64]{1,0:T(8,128)}, u32[]{:S(2)}) copy-start(f32[8,64]{1,0:T(8,128)} %get-tuple-element.3455) | copy-start | bytes 6148 | tf_op jit(solution)/shard_map/while
  407.2 26.6 %copy-start.76 = (f32[8,64]{1,0:T(8,128)S(1)}, f32[8,64]{1,0:T(8,128)}, u32[]{:S(2)}) copy-start(f32[8,64]{1,0:T(8,128)} %get-tuple-element.3456) | copy-start | bytes 6148 | tf_op jit(solution)/shard_map/while
  473.2 25.0 %copy-start.60 = (f32[8,64]{1,0:T(8,128)S(1)}, f32[8,64]{1,0:T(8,128)}, u32[]{:S(2)}) copy-start(f32[8,64]{1,0:T(8,128)} %get-tuple-element.3447) | copy-start | bytes 6148 | tf_op jit(solution)/shard_map/while
  473.2 25.0 %copy-start.64 = (f32[8,64]{1,0:T(8,128)S(1)}, f32[8,64]{1,0:T(8,128)}, u32[]{:S(2)}) copy-start(f32[8,64]{1,0:T(8,128)} %get-tuple-element.3448) | copy-start | bytes 6148 | tf_op jit(solution)/shard_map/while
  473.4 26.2 %copy-start.55 = (f32[8,64]{1,0:T(8,128)S(1)}, f32[8,64]{1,0:T(8,128)}, u32[]{:S(2)}) copy-start(f32[8,64]{1,0:T(8,128)} %get-tuple-element.3445) | copy-start | bytes 6148 | tf_op jit(solution)/shard_map/while
  473.4 26.1 %copy-start.59 = (f32[8,64]{1,0:T(8,128)S(1)}, f32[8,64]{1,0:T(8,128)}, u32[]{:S(2)}) copy-start(f32[8,64]{1,0:T(8,128)} %get-tuple-element.3443) | copy-start | bytes 6148 | tf_op jit(solution)/shard_map/while
  473.4 26.1 %copy-start.63 = (f32[8,64]{1,0:T(8,128)S(1)}, f32[8,64]{1,0:T(8,128)}, u32[]{:S(2)}) copy-start(f32[8,64]{1,0:T(8,128)} %get-tuple-element.3444) | copy-start | bytes 6148 | tf_op jit(solution)/shard_map/while
  482.3 25.9 %copy-start.65 = (f32[8,64]{1,0:T(8,128)S(1)}, f32[8,64]{1,0:T(8,128)}, u32[]{:S(2)}) copy-start(f32[8,64]{1,0:T(8,128)} %get-tuple-element.3461) | copy-start | bytes 6148 | tf_op jit(solution)/shard_map/while
  482.3 25.9 %copy-start.70 = (f32[8,64]{1,0:T(8,128)S(1)}, f32[8,64]{1,0:T(8,128)}, u32[]{:S(2)}) copy-start(f32[8,64]{1,0:T(8,128)} %get-tuple-element.3459) | copy-start | bytes 6148 | tf_op jit(solution)/shard_map/while
  482.3 25.9 %copy-start.74 = (f32[8,64]{1,0:T(8,128)S(1)}, f32[8,64]{1,0:T(8,128)}, u32[]{:S(2)}) copy-start(f32[8,64]{1,0:T(8,128)} %get-tuple-element.3460) | copy-start | bytes 6148 | tf_op jit(solution)/shard_map/while
  482.3 26.6 %copy-start.68 = (f32[8,64]{1,0:T(8,128)S(1)}, f32[8,64]{1,0:T(8,128)}, u32[]{:S(2)}) copy-start(f32[8,64]{1,0:T(8,128)} %get-tuple-element.3457) | copy-start | bytes 6148 | tf_op jit(solution)/shard_map/while
  482.3 26.6 %copy-start.72 = (f32[8,64]{1,0:T(8,128)S(1)}, f32[8,64]{1,0:T(8,128)}, u32[]{:S(2)}) copy-start(f32[8,64]{1,0:T(8,128)} %get-tuple-element.3455) | copy-start | bytes 6148 | tf_op jit(solution)/shard_map/while
  482.3 26.6 %copy-start.76 = (f32[8,64]{1,0:T(8,128)S(1)}, f32[8,64]{1,0:T(8,128)}, u32[]{:S(2)}) copy-start(f32[8,64]{1,0:T(8,128)} %get-tuple-element.3456) | copy-start | bytes 6148 | tf_op jit(solution)/shard_map/while
  (386 other events, 5798.9 us)
Sparse Core Ops, SparseCore 0:
  191.8 53.0 all-gather.8
  247.0 49.3 all-gather.10
  298.5 49.2 all-gather.12
  541.2 53.1 all-gather.14
where the time goes:
time: 1530 us; the launch traced here: 1520 us
  other arithmetic  825 us (54%)
  matrix products  527 us (34%)
  local copies, waits for them, and re-layouts  95.2 us (6%)
  loops' own time  61.3 us (4%)
    while x248, other arithmetic  543 us
    dot_general x256, matrix products, retreat(): along = jnp.einsum('hvk,hk->hv', adjoint, erase_dir, precision=HIGHEST)  248 us
    dot_general x256, matrix products, advance(): along = jnp.einsum('hvk,hk->hv', state, unit_kappa, precision=HIGHEST)  218 us
    add x28, other arithmetic, backward_exact(): adjoint = carry + rank_one(block[6][within], block[3][within])  89 us
    add x28, other arithmetic, backward_totals(): adjoint = carry + rank_one(block[6][within], block[3][within])  87.3 us
    sub x8, other arithmetic, retreat(): adjoint * decays[:, None, :] - along[:, :, None] * unit_kappa[:, None, :]  52.5 us
    another operation x1, loops' own time, local(): carry_back, unused = lax.scan(backward_totals, blank, series, reverse=True)  48 us
  transfers between devices with their start and end apart: 4, of which 0 were waited for; matrix products, arithmetic and copies ran while one was open for 37% of the time, Pallas kernels for 0%

commit v1 on v0

v1 whole, which is shorter than its diff:
```python
import functools

import jax
import jax.numpy as jnp
from jax import lax
from jax.experimental import pallas as pl
from jax.experimental.pallas import tpu as pltpu
from jax.sharding import PartitionSpec as P

H = 8
HS = 64
F32 = jnp.float32
BF16 = jnp.bfloat16
NN = (((1,), (0,)), ((), ()))
NT = (((1,), (1,)), ((), ()))


def halves(a):
    high = a.astype(BF16)
    return high, (a - high.astype(F32)).astype(BF16)


def dot3(a, b, dims=NN):
    ah, al = a if isinstance(a, tuple) else halves(a)
    bh, bl = b if isinstance(b, tuple) else halves(b)
    one = functools.partial(lax.dot_general, dimension_numbers=dims, preferred_element_type=F32)
    return one(ah, bh) + (one(ah, bl) + one(al, bh))


def iota(shape, dim):
    return lax.broadcasted_iota(jnp.int32, shape, dim)


def local_kernel(
    len_ref, r_ref, k_ref, v_ref, kap_ref, rem_ref, rate_ref, g_ref,
    rows_ref, maps_ref, xy_ref, w_ref, vg_ref,
):
    T, C = r_ref.shape
    live = (iota((T, 1), 0) < len_ref[0]).astype(F32)
    left = iota((T, 2 * HS), 1) < HS
    units = []
    for p in range(C // (2 * HS)):
        kap = kap_ref[:, p * 128:(p + 1) * 128].astype(F32)
        sq = kap * kap
        sa = jnp.sum(jnp.where(left, sq, 0.0), axis=1, keepdims=True)
        sb = jnp.sum(jnp.where(left, 0.0, sq), axis=1, keepdims=True)
        units.append(kap / jnp.sqrt(jnp.where(left, sa, sb) + 1e-05))
    kap = jnp.concatenate(units, axis=1)
    rate = rate_ref[...] * live
    e = rem_ref[...].astype(F32) * live * kap
    r = r_ref[...].astype(F32) * live
    k = k_ref[...].astype(F32) * live
    v = v_ref[...].astype(F32) * live
    g = g_ref[...].astype(F32) * live
    rows_ref[0] = jnp.exp(-rate)
    rows_ref[1] = kap
    rows_ref[2] = e
    rows_ref[3] = r
    rows_ref[4] = k
    tril = (iota((T, T), 0) >= iota((T, T), 1)).astype(F32)
    cs = lax.dot_general(tril, rate, NN, precision=lax.Precision.HIGHEST, preferred_element_type=F32)
    mid = cs[T // 2 - 1:T // 2, :]
    end = cs[T - 1:T, :]
    grow = jnp.exp(cs - mid)
    kap_c = kap * jnp.exp(mid - cs + rate)
    r_c = r * jnp.exp(mid - cs)
    e_ct = (e * grow).T
    k_ct = (k * grow).T
    kap_0t = (kap * jnp.exp(rate - cs)).T
    r_0t = (r * jnp.exp(-cs)).T
    to_end = jnp.exp(cs - end)
    e_end = e * to_end
    k_end = k * to_end
    e_endt = e_end.T
    vt = v.T
    gt = g.T
    vg_ref[0] = vt
    vg_ref[1] = gt
    whole = jnp.exp(-end)
    strict = iota((T, T), 0) > iota((T, T), 1)
    lower = iota((T, T), 0) >= iota((T, T), 1)
    eye = (iota((T, T), 0) == iota((T, T), 1)).astype(F32)
    eye_h = (iota((HS, HS), 0) == iota((HS, HS), 1)).astype(F32)
    heads = range(C // HS)
    row = lambda a, h: a[:, h * HS:(h + 1) * HS]
    col = lambda a, h: a[h * HS:(h + 1) * HS, :]
    low, mixes, seen = [], [], []
    for h in heads:
        both = dot3(
            jnp.concatenate([row(kap_c, h), row(r_c, h)], axis=0),
            jnp.concatenate([col(e_ct, h), col(k_ct, h)], axis=1),
        )
        low.append(jnp.where(strict, both[:T, :T], 0.0))
        mixes.append(jnp.where(strict, both[:T, T:], 0.0))
        seen.append(jnp.where(lower, both[T:, :T], 0.0))
    inverse = [eye - m for m in low]
    power = low
    size = 2
    while size < T:
        split = [halves(m) for m in power]
        power = [dot3(s, s) for s in split]
        inverse = [i + dot3(i, m) for i, m in zip(inverse, power)]
        size *= 2
    bs = []
    for h in heads:
        inv = halves(inverse[h])
        q = halves(seen[h])
        nvt = dot3(col(vt, h), mixes[h], NT)
        xy = dot3(jnp.concatenate([col(kap_0t, h), nvt], axis=0), inv, NT)
        xy_ref[h] = xy
        pa = dot3(xy, row(e_end, h))
        a = dot3(col(vt, h), row(k_end, h)) - pa[HS:]
        prod = eye_h * row(whole, h) - pa[:HS]
        maps_ref[h] = jnp.concatenate([prod, a], axis=1)
        zt = col(r_0t, h) - dot3(xy[:HS], q, NT)
        bs.append(dot3(col(gt, h), zt, NT))
        gq = dot3(col(gt, h), q)
        w_ref[h] = dot3(jnp.concatenate([col(e_endt, h), gq], axis=0), inv)
    for p in range(len(bs) // 2):
        maps_ref[len(bs) + p] = jnp.concatenate([bs[2 * p], bs[2 * p + 1]], axis=1)


def exact_kernel(
    place_ref, gath_ref, rows_ref, xy_ref, w_ref, vg_ref, gx_ref, vx_ref,
    mix_ref, gr_ref, gk_ref, gv_ref,
    sf, sb, st, lt, packs, lowf, lowb, gr_acc, gk_acc,
):
    T, C = gr_ref.shape
    pairs = C // 128
    heads = C // HS
    count = gath_ref.shape[0]
    me = place_ref[0]
    sf[...] = jnp.zeros_like(sf)
    sb[...] = jnp.zeros_like(sb)

    def ahead(i, _):
        for h in range(heads):
            pa = gath_ref[i, h]
            sf[h] = dot3(sf[h], pa[:, :HS]) + pa[:, HS:]
        return 0

    lax.fori_loop(0, me, ahead, 0)

    def behind(i, _):
        at = count - 1 - i
        for h in range(heads):
            pa = gath_ref[at, h]
            b = gath_ref[at, heads + h // 2][:, (h % 2) * HS:(h % 2 + 1) * HS]
            sb[h] = dot3(sb[h], pa[:, :HS], NT) + b
        return 0

    lax.fori_loop(0, count - 1 - me, behind, 0)

    lane_left = iota((HS, 128), 1) < HS

    def pack(which, p, a, b):
        packs[which, 0, p] = jnp.where(lane_left, a, pltpu.roll(b, HS, 1))
        packs[which, 1, p] = jnp.where(lane_left, pltpu.roll(a, HS, 1), b)

    for p in range(pairs):
        ha, hb = 2 * p, 2 * p + 1
        along = [dot3(sf[h], xy_ref[h, :HS]) + xy_ref[h, HS:] for h in (ha, hb)]
        beta = [dot3(sb[h], w_ref[h, :HS]) + w_ref[h, HS:] for h in (ha, hb)]
        pack(0, p, *along)
        pack(1, p, *beta)
        pack(2, p, *[vg_ref[0, h * HS:(h + 1) * HS, :] for h in (ha, hb)])
        pack(3, p, *[vg_ref[1, h * HS:(h + 1) * HS, :] for h in (ha, hb)])
        st[p] = jnp.concatenate([sf[ha], sf[hb]], axis=1)
        lt[p] = jnp.concatenate([sb[ha], sb[hb]], axis=1)

    offset = jnp.where(lane_left, 0, HS)
    head_mask = (iota((8, C), 0) == iota((8, C), 1) // HS).astype(F32)
    own = iota((32, 256), 0) // 8 == iota((32, 256), 1) // HS

    def contract(base, low, by_key, left_ref, out_v, out_k):
        keys = rows_ref[by_key, pl.ds(base, 8), :]
        sums = []
        for part in range(2):
            rows32 = pl.ds(pl.multiple_of(base * 8 + part * 32, 32), 32)
            expanded = jnp.concatenate(
                [keys[j:j + 1, :] * head_mask for j in range(part * 4, part * 4 + 4)], axis=0
            ).astype(BF16)
            full = low[part * 256:(part + 1) * 256, :]
            ov = lax.dot_general(expanded, full, NT, preferred_element_type=F32)
            ov = jnp.where(own, ov, 0.0)
            ov = ov[:, :128] + ov[:, 128:]
            ov = ov + pltpu.roll(ov, HS, 1)
            out_v[rows32, :] = ov[:, :HS].astype(BF16)
            lhs = jnp.where(own, left_ref[rows32, :].astype(F32), 0.0).astype(BF16)
            ok = lax.dot_general(lhs, full, NN, preferred_element_type=F32)
            sums += [
                jnp.sum(ok[j * 8:(j + 1) * 8, :] * head_mask, axis=0, keepdims=True) for j in range(4)
            ]
        out_k[pl.ds(base, 8), :] = jnp.concatenate(sums, axis=0)

    def step(group, _):
        base = pl.multiple_of(group * 8, 8)
        base_b = pl.multiple_of(T - 8 - base, 8)
        half = base // HS
        half_b = base_b // HS
        at = offset + (base - half * HS)
        at_b = offset + (base_b - half_b * HS)
        spread = lambda a, i: jnp.take_along_axis(a, i, axis=1)
        for p in range(pairs):
            cols = slice(p * 128, (p + 1) * 128)
            rows = [rows_ref[n, pl.ds(base, 8), cols] for n in (0, 2, 4)]
            along, vals = packs[0, half, p], packs[2, half, p]
            s = st[p]
            for j in range(8):
                d, e, k = [a[j:j + 1, :] for a in rows]
                s = s * d - spread(along, at + j) * e + spread(vals, at + j) * k
                lowf[j * HS:(j + 1) * HS, cols] = s.astype(BF16)
            st[p] = s
            rows = [rows_ref[n, pl.ds(base_b, 8), cols] for n in (0, 1, 3)]
            beta, grads = packs[1, half_b, p], packs[3, half_b, p]
            c = lt[p]
            for j in reversed(range(8)):
                d, u, r = [a[j:j + 1, :] for a in rows]
                adj = c + spread(grads, at_b + j) * r
                lowb[j * HS:(j + 1) * HS, cols] = adj.astype(BF16)
                c = adj * d - spread(beta, at_b + j) * u
            lt[p] = c
        contract(base, lowf, 3, gx_ref, mix_ref, gr_acc)
        contract(base_b, lowb, 4, vx_ref, gv_ref, gk_acc)
        return 0

    lax.fori_loop(0, T // 8, step, 0)
    gr_ref[...] = gr_acc[...].astype(BF16)
    gk_ref[...] = gk_acc[...].astype(BF16)


def local(receptance, token_key, token_value, kappa_raw, removal, decay_rate, shard_length, grad_output):
    T, C = receptance.shape
    heads = C // HS
    vmem = pl.BlockSpec(memory_space=pltpu.VMEM)
    smem = pl.BlockSpec(memory_space=pltpu.SMEM)
    sds = jax.ShapeDtypeStruct
    rows, maps, xy, w, vg = pl.pallas_call(
        local_kernel,
        out_shape=(
            sds((5, T, C), F32),
            sds((heads + heads // 2, HS, 2 * HS), F32),
            sds((heads, 2 * HS, T), F32),
            sds((heads, 2 * HS, T), F32),
            sds((2, C, T), F32),
        ),
        in_specs=[smem] + [vmem] * 7,
        out_specs=(vmem,) * 5,
        compiler_params=pltpu.CompilerParams(vmem_limit_bytes=48 * 1024 * 1024),
    )(shard_length, receptance, token_key, token_value, kappa_raw, removal, decay_rate, grad_output)
    gathered = lax.all_gather(maps, "ctx")
    place = lax.axis_index("ctx").astype(jnp.int32).reshape(1)
    live = lax.broadcasted_iota(jnp.int32, (T, 1), 0) < shard_length[0]

    def spread(a):
        a = jnp.where(live, a, jnp.zeros_like(a)).reshape(T * heads, HS)
        return jnp.tile(a, (1, 4))

    mix, gr, gk, gv = pl.pallas_call(
        exact_kernel,
        out_shape=(
            sds((T * heads, HS), BF16),
            sds((T, C), BF16),
            sds((T, C), BF16),
            sds((T * heads, HS), BF16),
        ),
        in_specs=[smem] + [vmem] * 7,
        out_specs=(vmem,) * 4,
        scratch_shapes=[
            pltpu.VMEM((heads, HS, HS), F32),
            pltpu.VMEM((heads, HS, HS), F32),
            pltpu.VMEM((heads // 2, HS, 2 * HS), F32),
            pltpu.VMEM((heads // 2, HS, 2 * HS), F32),
            pltpu.VMEM((4, 2, heads // 2, HS, 2 * HS), F32),
            pltpu.VMEM((8 * HS, C), BF16),
            pltpu.VMEM((8 * HS, C), BF16),
            pltpu.VMEM((T, C), F32),
            pltpu.VMEM((T, C), F32),
        ],
        compiler_params=pltpu.CompilerParams(vmem_limit_bytes=56 * 1024 * 1024),
    )(place, gathered, rows, xy, w, vg, spread(grad_output), spread(token_value))
    return mix.reshape(T, C), gr, gk, gv.reshape(T, C)


def solution(mesh):
    both = P(("dp", "ctx"), None)
    return jax.shard_map(
        local,
        mesh=mesh,
        in_specs=(both,) * 6 + (P(("dp", "ctx")), both),
        out_specs=(both,) * 4,
        check_vma=False,
    )
```

time: 1530 us -> 144 us (0.09)
  other arithmetic: 825 us -> 1.06 us
  matrix products: 527 us -> 0 us
  local copies, waits for them, and re-layouts: 95.2 us -> 16.3 us
  loops' own time: 61.3 us -> 0 us
  waiting for transfers between devices: 0.75 us -> 60.7 us
  Pallas kernels: 0 us -> 50.5 us
    while x248 -> x0, other arithmetic: 543 us -> none
    dot_general x543 -> x0, matrix products: 527 us -> none  [the longest x256 248 us: retreat(): along = jnp.einsum('hvk,hk->hv', adjoint, erase_dir, precision=HIGHEST)]
    add x120 -> x0, other arithmetic: 200 us -> none  [the longest x28 89 us: backward_exact(): adjoint = carry + rank_one(block[6][within], block[3][within])]
    another operation x6 -> x0, loops' own time: 61.3 us -> none  [the longest x1 48 us: local(): carry_back, unused = lax.scan(backward_totals, blank, series, reverse=True)]
    all_gather x4 -> x1, waiting for transfers between devices: 0.01 us -> 60.6 us  [local(): gathered = lax.all_gather(maps, 'ctx')]
    sub x8 -> x0, other arithmetic: 52.5 us -> none  [retreat(): adjoint * decays[:, None, :] - along[:, :, None] * unit_kappa[:, None, :]]
    pallas_call x0 -> x2, Pallas kernels: none -> 50.5 us  [the longest x1 39.8 us: local(): pl.pallas_call(exact_kernel, out_shape=(sds((T * heads, HS), BF16), sds((...]
    mul x84 -> x0, local copies, waits for them, and re-layouts: 38.9 us -> none  [the longest x48 24.3 us: rank_one(): return left[:, :, None] * right[:, None, :]]
  transfers between devices with their start and end apart: 4 -> 1, of which waited for: 0 -> 1; matrix products, arithmetic and copies ran while one was open for 37% -> 3% of each run, Pallas kernels for 0% -> 0%
where the time goes in v1:
time: 144 us; the launch traced here: 143 us
  waiting for transfers between devices  60.7 us (42%)
  Pallas kernels  50.5 us (35%)
  local copies, waits for them, and re-layouts  16.3 us (11%)
  between operations  14.8 us (10%)
    all_gather x1, waiting for transfers between devices, local(): gathered = lax.all_gather(maps, 'ctx')  60.6 us
    pallas_call x1, Pallas kernels, local(): pl.pallas_call(exact_kernel, out_shape=(sds((T * heads, HS), BF16), sds((...  39.8 us
    pallas_call x1, Pallas kernels, local(): pl.pallas_call(local_kernel, out_shape=(sds((5, T, C), F32), sds((heads +...  10.7 us
    unnamed x22, local copies, waits for them, and re-layouts  9.95 us
    reshape x2, local copies, waits for them, and re-layouts, local(): return (mix.reshape(T, C), gr, gk, gv.reshape(T, C))  3.64 us
  transfers between devices with their start and end apart: 1, of which 1 were waited for; matrix products, arithmetic and copies ran while one was open for 3% of the time, Pallas kernels for 0%

profile of v1, /device:TPU:1, one launch (start us, length us, event | category | flops | bytes accessed | tf_op | source)
XLA Modules:
  0.0 143.3 jit_solution(4959544666355655417)
XLA Ops:
  7.2 0.0 all-gather.3.cloned.1.call-start
  7.9 0.0 copy-start.4
  7.9 0.9 copy-done.4
  8.8 0.0 copy-start.5
  8.8 0.9 copy-done.5
  9.7 0.0 copy-start.6
  9.7 0.9 copy-done.6
  10.6 0.0 copy-start.7
  10.6 0.9 copy-done.7
  11.5 0.0 copy-start.8
  11.5 0.9 copy-done.8
  12.4 0.0 copy-start.9
  12.4 0.9 copy-done.9
  13.3 0.0 copy-start.10
  13.3 0.9 copy-done.10
  14.2 10.7 %shard_map.111 = (f32[5,128,512]{2,1,0:T(8,128)S(1)}, f32[12,64,128]{2,1,0:T(8,128)}, f32[8,128,128]{2,1,0:T(8,128)S(1)}, f32[8,128,128]{2,1,0:T(8,128)S(1)}, f32[2,512,128]{2,1,0:T(8,128)S(1)}) custom-call(s32[1]{0:T(128)} %copy.20.len_ref, bf16[128,512]{1,0:T(8,128)(2,1)S(1)} %copy-done.7, bf16[128,512]{1,0:T(8,128)(2,1)S(1)} %copy-done.8, ...), custom_call_target="tpu_custom_call" | custom-call | tf_op jit(solution)/shard_map/pallas_call | solution.py:238
  24.9 0.0 copy-start
  24.9 1.0 copy-done
  26.0 0.0 copy-start.1
  26.0 0.8 copy-done.1
  26.8 0.0 copy-start.2
  26.8 0.8 copy-done.2
  27.7 0.0 copy-start.3
  27.7 0.9 copy-done.3
  28.5 0.0 all-gather.3.cloned.1.call-update
  28.6 1.1 broadcast_select_fusion
  29.6 0.2 tile.23
  29.8 0.1 copy.17
  30.0 0.2 tile.20
  30.2 0.1 copy.16
  30.3 0.1 tile.21
  30.4 1.0 copy.18.gx_ref
  31.4 1.0 copy.19.vx_ref
  32.4 60.6 %all-gather.3.cloned.1.call-done = f32[192,64,128]{2,1,0:T(8,128)} async-done(((f32[12,64,128]{2,1,0:T(8,128)}), f32[192,64,128]{2,1,0:T(8,128)}) %all-gather.3.cloned.1.call-update) | async-done | bytes 6291472 | tf_op jit(solution)/shard_map/all_gather | solution.py:251
  93.1 39.8 %shard_map.112 = (bf16[1024,64]{1,0:T(8,128)(2,1)}, bf16[128,512]{1,0:T(8,128)(2,1)}, bf16[128,512]{1,0:T(8,128)(2,1)}, bf16[1024,64]{1,0:T(8,128)(2,1)}) custom-call(s32[1]{0:T(128)} %bitcast.place_ref, f32[16,12,64,128]{3,2,1,0:T(8,128)} %bitcast.6, f32[5,128,512]{2,1,0:T(8,128)} %copy-done, f32[8,128,128]{2,1,0:T(8,128)} %copy-done.1, ...), custom_call_target="tpu_custom_call" | custom-call | tf_op jit(solution)/shard_map/pallas_call | solution.py:259
  132.8 1.8 %reshape.31 = bf16[128,512]{1,0:T(8,128)(2,1)} reshape(bf16[1024,64]{1,0:T(8,128)(2,1)} %get-tuple-element.18) | data formatting | bytes 262144 | tf_op jit(solution)/shard_map/reshape | solution.py:282
  134.6 1.8 %reshape.32 = bf16[128,512]{1,0:T(8,128)(2,1)} reshape(bf16[1024,64]{1,0:T(8,128)(2,1)} %get-tuple-element.21) | data formatting | bytes 262144 | tf_op jit(solution)/shard_map/reshape | solution.py:282
  (2 shorter events, 0.1 us)
Async XLA Ops:
  7.2 85.9 %all-gather.3.cloned.1.call-start = ((), (), s32[]{:S(2)}) async-start(), calls=%async_computation | async-start | bytes 6684672 | tf_op jit(solution)/shard_map/all_gather | solution.py:251
  7.9 0.9 copy-start.4
  8.8 0.9 copy-start.5
  9.7 0.9 copy-start.6
  10.6 0.9 copy-start.7
  11.5 0.9 copy-start.8
  12.4 0.9 copy-start.9
  13.3 0.9 copy-start.10
  24.9 1.1 copy-start
  26.0 0.8 copy-start.1
  26.8 0.8 copy-start.2
  27.7 0.9 copy-start.3
Sparse Core Ops, SparseCore 0:
  28.7 64.3 all-gather.2

commit v2 on v1

--- a/solution.py
+++ b/solution.py
@@ -32,9 +32,18 @@
 
 
 def local_kernel(
-    len_ref, r_ref, k_ref, v_ref, kap_ref, rem_ref, rate_ref, g_ref,
-    rows_ref, maps_ref, xy_ref, w_ref, vg_ref,
+    len_ref, *refs,
 ):
+    sources, (rows_ref, maps_ref, xy_ref, w_ref, vg_ref) = refs[:7], refs[7:12]
+    staged, sems = refs[12:19], refs[19]
+    copies = [
+        pltpu.make_async_copy(src, dst, sems.at[i]) for i, (src, dst) in enumerate(zip(sources, staged))
+    ]
+    for copy in copies:
+        copy.start()
+    for copy in copies:
+        copy.wait()
+    r_ref, k_ref, v_ref, kap_ref, rem_ref, rate_ref, g_ref = staged
     T, C = r_ref.shape
     live = (iota((T, 1), 0) < len_ref[0]).astype(F32)
     left = iota((T, 2 * HS), 1) < HS
@@ -57,6 +66,8 @@
     rows_ref[2] = e
     rows_ref[3] = r
     rows_ref[4] = k
+    rows_ref[5] = v
+    rows_ref[6] = g
     tril = (iota((T, T), 0) >= iota((T, T), 1)).astype(F32)
     cs = lax.dot_general(tril, rate, NN, precision=lax.Precision.HIGHEST, preferred_element_type=F32)
     mid = cs[T // 2 - 1:T // 2, :]
@@ -101,7 +112,7 @@
         power = [dot3(s, s) for s in split]
         inverse = [i + dot3(i, m) for i, m in zip(inverse, power)]
         size *= 2
-    bs = []
+    maps = []
     for h in heads:
         inv = halves(inverse[h])
         q = halves(seen[h])
@@ -111,46 +122,111 @@
         pa = dot3(xy, row(e_end, h))
         a = dot3(col(vt, h), row(k_end, h)) - pa[HS:]
         prod = eye_h * row(whole, h) - pa[:HS]
-        maps_ref[h] = jnp.concatenate([prod, a], axis=1)
         zt = col(r_0t, h) - dot3(xy[:HS], q, NT)
-        bs.append(dot3(col(gt, h), zt, NT))
+        maps.append((a, prod, dot3(col(gt, h), zt, NT)))
         gq = dot3(col(gt, h), q)
         w_ref[h] = dot3(jnp.concatenate([col(e_endt, h), gq], axis=0), inv)
-    for p in range(len(bs) // 2):
-        maps_ref[len(bs) + p] = jnp.concatenate([bs[2 * p], bs[2 * p + 1]], axis=1)
+    for p in range(len(maps) // 2):
+        for i in range(3):
+            maps_ref[p, i] = jnp.concatenate([maps[2 * p][i], maps[2 * p + 1][i]], axis=1)
+
+
+def carry_kernel(
+    count, maps_ref, out_ref, member, group, incoming, states, ready,
+    s1, r1, s2, r2, s3, r3,
+):
+    size = maps_ref.shape[0]
+    groups = count // size
+    me = lax.axis_index("ctx")
+    q = me % size
+    z = me // size
+    peers = [z * size + (q + d) % size for d in range(1, size)]
+    others = [((z + d) % groups) * size + q for d in range(1, groups)]
+    barrier = pltpu.get_barrier_semaphore()
+    for device in peers + others:
+        pl.semaphore_signal(barrier, inc=1, device_id={"ctx": device}, device_id_type=pl.DeviceIdType.MESH)
+    pl.semaphore_wait(barrier, len(peers) + len(others))
+
+    def send(src, dst, send_sem, recv_sem, device):
+        copy = pltpu.make_async_remote_copy(
+            src_ref=src, dst_ref=dst, send_sem=send_sem, recv_sem=recv_sem,
+            device_id={"ctx": device}, device_id_type=pl.DeviceIdType.MESH,
+        )
+        copy.start()
+        return copy
+
+    first = [
+        send(maps_ref.at[(q + d) % size], member.at[q], s1.at[d - 1], r1.at[d - 1], peers[d - 1])
+        for d in range(1, size)
+    ]
+    member[q] = maps_ref[q]
+    for copy in first:
+        copy.wait_recv()
+    left = iota((HS, 2 * HS), 1) < HS
+
+    def spread(m):
+        return halves(jnp.concatenate([jnp.where(left, m, 0.0), jnp.where(left, 0.0, m)], axis=0))
+
+    blocks = [spread(member[m, 1]) for m in range(size)]
+    ahead = jnp.concatenate([member[0, 0], member[0, 1]], axis=0)
+    back = member[size - 1, 2]
+    for m in range(1, size):
+        ahead = dot3(ahead, blocks[m])
+        ahead = jnp.concatenate([ahead[:HS] + member[m, 0], ahead[HS:]], axis=0)
+        n = size - 1 - m
+        back = dot3(back, blocks[n], NT) + member[n, 2]
+    group[0] = ahead[:HS]
+    group[1] = ahead[HS:]
+    group[2] = back
+    second = []
+    for d in range(1, groups):
+        part = pl.ds((z + d) // groups, 2)
+        second.append(
+            send(group.at[part], incoming.at[z, part], s2.at[d - 1], r2.at[d - 1], others[d - 1])
+        )
+    for copy in second:
+        copy.wait_recv()
+
+    ready[...] = jnp.zeros_like(ready)
+
+    def forward(i, _):
+        ready[0] = dot3(ready[0], spread(incoming[i, 1])) + incoming[i, 0]
+        return 0
+
+    lax.fori_loop(0, z, forward, 0)
+
+    def backward(i, _):
+        at = groups - 1 - i
+        ready[1] = dot3(ready[1], spread(incoming[at, 1]), NT) + incoming[at, 2]
+        return 0
+
+    lax.fori_loop(0, groups - 1 - z, backward, 0)
+    state, adjoint = ready[0], ready[1]
+    for m in range(size):
+        n = size - 1 - m
+        states[m, 0] = state
+        states[n, 1] = adjoint
+        if m < size - 1:
+            state = dot3(state, blocks[m]) + member[m, 0]
+            adjoint = dot3(adjoint, blocks[n], NT) + member[n, 2]
+    third = [
+        send(states.at[(q + d) % size], out_ref.at[q], s3.at[d - 1], r3.at[d - 1], peers[d - 1])
+        for d in range(1, size)
+    ]
+    out_ref[q] = states[q]
+    for copy in third:
+        copy.wait_recv()
+    for copy in first + second + third:
+        copy.wait_send()
 
 
 def exact_kernel(
-    place_ref, gath_ref, rows_ref, xy_ref, w_ref, vg_ref, gx_ref, vx_ref,
+    carry_ref, rows_ref, xy_ref, w_ref, vg_ref,
     mix_ref, gr_ref, gk_ref, gv_ref,
-    sf, sb, st, lt, packs, lowf, lowb, gr_acc, gk_acc,
+    st, lt, packs, lowf, lowb, mix_acc, gr_acc, gk_acc, gv_acc,
 ):
     T, C = gr_ref.shape
     pairs = C // 128
-    heads = C // HS
-    count = gath_ref.shape[0]
-    me = place_ref[0]
-    sf[...] = jnp.zeros_like(sf)
-    sb[...] = jnp.zeros_like(sb)
-
-    def ahead(i, _):
-        for h in range(heads):
-            pa = gath_ref[i, h]
-            sf[h] = dot3(sf[h], pa[:, :HS]) + pa[:, HS:]
-        return 0
-
-    lax.fori_loop(0, me, ahead, 0)
-
-    def behind(i, _):
-        at = count - 1 - i
-        for h in range(heads):
-            pa = gath_ref[at, h]
-            b = gath_ref[at, heads + h // 2][:, (h % 2) * HS:(h % 2 + 1) * HS]
-            sb[h] = dot3(sb[h], pa[:, :HS], NT) + b
-        return 0
-
-    lax.fori_loop(0, count - 1 - me, behind, 0)
-
     lane_left = iota((HS, 128), 1) < HS
 
     def pack(which, p, a, b):
@@ -159,39 +235,50 @@
 
     for p in range(pairs):
         ha, hb = 2 * p, 2 * p + 1
-        along = [dot3(sf[h], xy_ref[h, :HS]) + xy_ref[h, HS:] for h in (ha, hb)]
-        beta = [dot3(sb[h], w_ref[h, :HS]) + w_ref[h, HS:] for h in (ha, hb)]
+        state, adjoint = carry_ref[p, 0], carry_ref[p, 1]
+        cut = lambda a: (a[:, :HS], a[:, HS:])
+        along = [dot3(s, xy_ref[h, :HS]) + xy_ref[h, HS:] for s, h in zip(cut(state), (ha, hb))]
+        beta = [dot3(s, w_ref[h, :HS]) + w_ref[h, HS:] for s, h in zip(cut(adjoint), (ha, hb))]
         pack(0, p, *along)
         pack(1, p, *beta)
         pack(2, p, *[vg_ref[0, h * HS:(h + 1) * HS, :] for h in (ha, hb)])
         pack(3, p, *[vg_ref[1, h * HS:(h + 1) * HS, :] for h in (ha, hb)])
-        st[p] = jnp.concatenate([sf[ha], sf[hb]], axis=1)
-        lt[p] = jnp.concatenate([sb[ha], sb[hb]], axis=1)
+        st[p] = state
+        lt[p] = adjoint
 
     offset = jnp.where(lane_left, 0, HS)
     head_mask = (iota((8, C), 0) == iota((8, C), 1) // HS).astype(F32)
     own = iota((32, 256), 0) // 8 == iota((32, 256), 1) // HS
 
-    def contract(base, low, by_key, left_ref, out_v, out_k):
+    def contract(base, low, by_key, by_value, out_v, out_k):
         keys = rows_ref[by_key, pl.ds(base, 8), :]
-        sums = []
+        values = rows_ref[by_value, pl.ds(base, 8), :]
+        sums_k, sums_v = [], []
         for part in range(2):
-            rows32 = pl.ds(pl.multiple_of(base * 8 + part * 32, 32), 32)
-            expanded = jnp.concatenate(
-                [keys[j:j + 1, :] * head_mask for j in range(part * 4, part * 4 + 4)], axis=0
-            ).astype(BF16)
+            spread_k, spread_v = [], []
+            for j in range(part * 4, part * 4 + 4):
+                spread_k.append(keys[j:j + 1, :] * head_mask)
+                v8 = values[j:j + 1, :] * head_mask
+                v8 = (v8[:, :128] + v8[:, 128:256]) + (v8[:, 256:384] + v8[:, 384:])
+                v8 = v8 + pltpu.roll(v8, HS, 1)
+                spread_v.append(jnp.concatenate([v8, v8], axis=1))
             full = low[part * 256:(part + 1) * 256, :]
-            ov = lax.dot_general(expanded, full, NT, preferred_element_type=F32)
+            ov = lax.dot_general(
+                jnp.concatenate(spread_k, axis=0).astype(BF16), full, NT, preferred_element_type=F32
+            )
             ov = jnp.where(own, ov, 0.0)
             ov = ov[:, :128] + ov[:, 128:]
             ov = ov + pltpu.roll(ov, HS, 1)
-            out_v[rows32, :] = ov[:, :HS].astype(BF16)
-            lhs = jnp.where(own, left_ref[rows32, :].astype(F32), 0.0).astype(BF16)
+            ov = jnp.concatenate([ov] * pairs, axis=1)
+            lhs = jnp.where(own, jnp.concatenate(spread_v, axis=0), 0.0).astype(BF16)
             ok = lax.dot_general(lhs, full, NN, preferred_element_type=F32)
-            sums += [
-                jnp.sum(ok[j * 8:(j + 1) * 8, :] * head_mask, axis=0, keepdims=True) for j in range(4)
-            ]
-        out_k[pl.ds(base, 8), :] = jnp.concatenate(sums, axis=0)
+            for sums, o in ((sums_k, ok), (sums_v, ov)):
+                sums += [
+                    jnp.sum(o[j * 8:(j + 1) * 8, :] * head_mask, axis=0, keepdims=True)
+                    for j in range(4)
+                ]
+        out_k[pl.ds(base, 8), :] = jnp.concatenate(sums_k, axis=0)
+        out_v[pl.ds(base, 8), :] = jnp.concatenate(sums_v, axis=0)
 
     def step(group, _):
         base = pl.multiple_of(group * 8, 8)
@@ -220,13 +307,15 @@
                 lowb[j * HS:(j + 1) * HS, cols] = adj.astype(BF16)
                 c = adj * d - spread(beta, at_b + j) * u
             lt[p] = c
-        contract(base, lowf, 3, gx_ref, mix_ref, gr_acc)
-        contract(base_b, lowb, 4, vx_ref, gv_ref, gk_acc)
+        contract(base, lowf, 3, 6, mix_acc, gr_acc)
+        contract(base_b, lowb, 4, 5, gv_acc, gk_acc)
         return 0
 
     lax.fori_loop(0, T // 8, step, 0)
     gr_ref[...] = gr_acc[...].astype(BF16)
     gk_ref[...] = gk_acc[...].astype(BF16)
+    mix_ref[...] = mix_acc[...].astype(BF16)
+    gv_ref[...] = gv_acc[...].astype(BF16)
 
 
 def local(receptance, token_key, token_value, kappa_raw, removal, decay_rate, shard_length, grad_output):
@@ -235,51 +324,58 @@
     vmem = pl.BlockSpec(memory_space=pltpu.VMEM)
     smem = pl.BlockSpec(memory_space=pltpu.SMEM)
     sds = jax.ShapeDtypeStruct
+    pairs = heads // 2
+    arrays = (receptance, token_key, token_value, kappa_raw, removal, decay_rate, grad_output)
     rows, maps, xy, w, vg = pl.pallas_call(
         local_kernel,
         out_shape=(
-            sds((5, T, C), F32),
-            sds((heads + heads // 2, HS, 2 * HS), F32),
+            sds((7, T, C), F32),
+            sds((pairs, 3, HS, 2 * HS), F32),
             sds((heads, 2 * HS, T), F32),
             sds((heads, 2 * HS, T), F32),
             sds((2, C, T), F32),
         ),
-        in_specs=[smem] + [vmem] * 7,
+        in_specs=[smem] + [pl.BlockSpec(memory_space=pltpu.MemorySpace.HBM)] * 7,
         out_specs=(vmem,) * 5,
-        compiler_params=pltpu.CompilerParams(vmem_limit_bytes=48 * 1024 * 1024),
-    )(shard_length, receptance, token_key, token_value, kappa_raw, removal, decay_rate, grad_output)
-    gathered = lax.all_gather(maps, "ctx")
-    place = lax.axis_index("ctx").astype(jnp.int32).reshape(1)
-    live = lax.broadcasted_iota(jnp.int32, (T, 1), 0) < shard_length[0]
-
-    def spread(a):
-        a = jnp.where(live, a, jnp.zeros_like(a)).reshape(T * heads, HS)
-        return jnp.tile(a, (1, 4))
-
-    mix, gr, gk, gv = pl.pallas_call(
+        scratch_shapes=[pltpu.VMEM((T, C), a.dtype) for a in arrays] + [pltpu.SemaphoreType.DMA((7,))],
+        compiler_params=pltpu.CompilerParams(vmem_limit_bytes=32 * 1024 * 1024),
+    )(shard_length, *arrays)
+    count = lax.axis_size("ctx")
+    groups = count // pairs
+    dma = pltpu.SemaphoreType.DMA
+    carry = pl.pallas_call(
+        functools.partial(carry_kernel, count),
+        out_shape=sds((pairs, 2, HS, 2 * HS), F32),
+        in_specs=[vmem],
+        out_specs=vmem,
+        scratch_shapes=[
+            pltpu.VMEM((pairs, 3, HS, 2 * HS), F32),
+            pltpu.VMEM((3, HS, 2 * HS), F32),
+            pltpu.VMEM((groups, 3, HS, 2 * HS), F32),
+            pltpu.VMEM((pairs, 2, HS, 2 * HS), F32),
+            pltpu.VMEM((2, HS, 2 * HS), F32),
+            dma((pairs - 1,)), dma((pairs - 1,)),
+            dma((groups - 1,)), dma((groups - 1,)),
+            dma((pairs - 1,)), dma((pairs - 1,)),
+        ],
+        compiler_params=pltpu.CompilerParams(
+            collective_id=0, has_side_effects=True, vmem_limit_bytes=32 * 1024 * 1024
+        ),
+    )(maps)
+    return pl.pallas_call(
         exact_kernel,
-        out_shape=(
-            sds((T * heads, HS), BF16),
-            sds((T, C), BF16),
-            sds((T, C), BF16),
-            sds((T * heads, HS), BF16),
-        ),
-        in_specs=[smem] + [vmem] * 7,
+        out_shape=(sds((T, C), BF16),) * 4,
+        in_specs=[vmem] * 5,
         out_specs=(vmem,) * 4,
         scratch_shapes=[
-            pltpu.VMEM((heads, HS, HS), F32),
-            pltpu.VMEM((heads, HS, HS), F32),
-            pltpu.VMEM((heads // 2, HS, 2 * HS), F32),
-            pltpu.VMEM((heads // 2, HS, 2 * HS), F32),
-            pltpu.VMEM((4, 2, heads // 2, HS, 2 * HS), F32),
+            pltpu.VMEM((pairs, HS, 2 * HS), F32),
+            pltpu.VMEM((pairs, HS, 2 * HS), F32),
+            pltpu.VMEM((4, 2, pairs, HS, 2 * HS), F32),
             pltpu.VMEM((8 * HS, C), BF16),
             pltpu.VMEM((8 * HS, C), BF16),
-            pltpu.VMEM((T, C), F32),
-            pltpu.VMEM((T, C), F32),
-        ],
-        compiler_params=pltpu.CompilerParams(vmem_limit_bytes=56 * 1024 * 1024),
-    )(place, gathered, rows, xy, w, vg, spread(grad_output), spread(token_value))
-    return mix.reshape(T, C), gr, gk, gv.reshape(T, C)
+        ] + [pltpu.VMEM((T, C), F32)] * 4,
+        compiler_params=pltpu.CompilerParams(vmem_limit_bytes=32 * 1024 * 1024),
+    )(carry, rows, xy, w, vg)
 
 
 def solution(mesh):

time: 144 us -> 73.1 us (0.51)
  waiting for transfers between devices: 60.7 us -> 0 us
  Pallas kernels: 50.5 us -> 65.2 us
  between operations: 14.8 us -> 1.31 us
  local copies, waits for them, and re-layouts: 16.3 us -> 6.37 us
    all_gather x1 -> x0, waiting for transfers between devices: 60.6 us -> none  [local(): gathered = lax.all_gather(maps, 'ctx')]
    pallas_call x2 -> x3, Pallas kernels: 50.5 us -> 65.2 us  [the longest x1 31.8 us: local(): pl.pallas_call(exact_kernel, out_shape=(sds((T, C), BF16),) * 4, in_specs...]
    reshape x2 -> x0, local copies, waits for them, and re-layouts: 3.64 us -> none  [local(): return (mix.reshape(T, C), gr, gk, gv.reshape(T, C))]
    unnamed x22 -> x14, local copies, waits for them, and re-layouts: 9.95 us -> 6.37 us
    another operation x8 -> x0, local copies, waits for them, and re-layouts: 2.73 us -> none  [spread(): return jnp.tile(a, (1, 4))]
  transfers between devices with their start and end apart: 1 -> 0, of which waited for: 1 -> 0; matrix products, arithmetic and copies ran while one was open for 3% -> 0% of each run, Pallas kernels for 0% -> 0%
where the time goes in v2:
time: 73.1 us; the launch traced here: 72.9 us
  Pallas kernels  65.2 us (89%)
  local copies, waits for them, and re-layouts  6.37 us (9%)
  between operations  1.31 us (2%)
    pallas_call x1, Pallas kernels, local(): pl.pallas_call(exact_kernel, out_shape=(sds((T, C), BF16),) * 4, in_specs...  31.8 us
    pallas_call x1, Pallas kernels, local(): pl.pallas_call(functools.partial(carry_kernel, count), out_shape=sds((pai...  22.3 us
    pallas_call x1, Pallas kernels, local(): pl.pallas_call(local_kernel, out_shape=(sds((7, T, C), F32), sds((pairs,...  11.1 us
    unnamed x14, local copies, waits for them, and re-layouts  6.37 us

profile of v2, /device:TPU:1, one launch (start us, length us, event | category | flops | bytes accessed | tf_op | source)
XLA Modules:
  0.0 72.9 jit_solution(17165790010863557719)
XLA Ops:
  1.3 0.0 copy-start
  1.3 0.9 %copy-done = f32[128,512]{1,0:T(8,128)S(1)} copy-done((f32[128,512]{1,0:T(8,128)S(1)}, f32[128,512]{1,0:T(8,128)}, u32[]{:S(2)}) %copy-start) | copy-done | bytes 262168
  2.2 0.0 copy-start.1
  2.2 0.9 %copy-done.1 = bf16[128,512]{1,0:T(8,128)(2,1)S(1)} copy-done((bf16[128,512]{1,0:T(8,128)(2,1)S(1)}, bf16[128,512]{1,0:T(8,128)(2,1)}, u32[]{:S(2)}) %copy-start.1) | copy-done | bytes 131096
  3.1 0.0 copy-start.2
  3.1 0.9 %copy-done.2 = bf16[128,512]{1,0:T(8,128)(2,1)S(1)} copy-done((bf16[128,512]{1,0:T(8,128)(2,1)S(1)}, bf16[128,512]{1,0:T(8,128)(2,1)}, u32[]{:S(2)}) %copy-start.2) | copy-done | bytes 131096
  4.0 0.0 copy-start.3
  4.0 0.9 %copy-done.3 = bf16[128,512]{1,0:T(8,128)(2,1)S(1)} copy-done((bf16[128,512]{1,0:T(8,128)(2,1)S(1)}, bf16[128,512]{1,0:T(8,128)(2,1)}, u32[]{:S(2)}) %copy-start.3) | copy-done | bytes 131096
  4.9 0.0 copy-start.4
  4.9 0.9 %copy-done.4 = bf16[128,512]{1,0:T(8,128)(2,1)S(1)} copy-done((bf16[128,512]{1,0:T(8,128)(2,1)S(1)}, bf16[128,512]{1,0:T(8,128)(2,1)}, u32[]{:S(2)}) %copy-start.4) | copy-done | bytes 131096
  5.8 0.0 copy-start.5
  5.9 0.9 %copy-done.5 = bf16[128,512]{1,0:T(8,128)(2,1)S(1)} copy-done((bf16[128,512]{1,0:T(8,128)(2,1)S(1)}, bf16[128,512]{1,0:T(8,128)(2,1)}, u32[]{:S(2)}) %copy-start.5) | copy-done | bytes 131096
  6.8 0.0 copy-start.6
  6.8 0.9 %copy-done.6 = bf16[128,512]{1,0:T(8,128)(2,1)S(1)} copy-done((bf16[128,512]{1,0:T(8,128)(2,1)S(1)}, bf16[128,512]{1,0:T(8,128)(2,1)}, u32[]{:S(2)}) %copy-start.6) | copy-done | bytes 131096
  7.7 11.1 %shard_map.111 = (f32[7,128,512]{2,1,0:T(8,128)S(1)}, f32[4,3,64,128]{3,2,1,0:T(8,128)S(1)}, f32[8,128,128]{2,1,0:T(8,128)S(1)}, f32[8,128,128]{2,1,0:T(8,128)S(1)}, f32[2,512,128]{2,1,0:T(8,128)S(1)}) custom-call(s32[1]{0:T(128)S(6)} %copy.12.len_ref, bf16[128,512]{1,0:T(8,128)(2,1)S(1)} %copy-done.1, bf16[128,512]{1,0:T(8,128)(2,1)S(1)} %copy-done.2, ...), custom_call_target="tpu_custom_call" | custom-call | tf_op jit(solution)/shard_map/pallas_call | solution.py:329
  18.8 22.3 %shard_map.112.carry_ref = f32[4,2,64,128]{3,2,1,0:T(8,128)S(1)} custom-call(f32[4,3,64,128]{3,2,1,0:T(8,128)S(1)} %get-tuple-element.9.maps_ref), custom_call_target="tpu_custom_call" | custom-call | tf_op jit(solution)/shard_map/pallas_call | solution.py:346
  41.1 31.8 %shard_map.113 = (bf16[128,512]{1,0:T(8,128)(2,1)}, bf16[128,512]{1,0:T(8,128)(2,1)}, bf16[128,512]{1,0:T(8,128)(2,1)}, bf16[128,512]{1,0:T(8,128)(2,1)}) custom-call(f32[4,2,64,128]{3,2,1,0:T(8,128)S(1)} %shard_map.112.carry_ref, f32[7,128,512]{2,1,0:T(8,128)S(1)} %get-tuple-element.10.rows_ref, f32[8,128,128]{2,1,0:T(8,128)S(1)} %get-tuple-element.11.xy_ref, ...), custom_call_target="tpu_custom_call" | custom-call | tf_op jit(solution)/shard_map/pallas_call | solution.py:365
Async XLA Ops:
  1.3 1.0 %copy-start = (f32[128,512]{1,0:T(8,128)S(1)}, f32[128,512]{1,0:T(8,128)}, u32[]{:S(2)}) copy-start(f32[128,512]{1,0:T(8,128)} %refs_5_.1) | copy-start | bytes 786436
  2.2 0.9 %copy-start.1 = (bf16[128,512]{1,0:T(8,128)(2,1)S(1)}, bf16[128,512]{1,0:T(8,128)(2,1)}, u32[]{:S(2)}) copy-start(bf16[128,512]{1,0:T(8,128)(2,1)} %refs_0_.1) | copy-start | bytes 393220
  3.1 0.9 %copy-start.2 = (bf16[128,512]{1,0:T(8,128)(2,1)S(1)}, bf16[128,512]{1,0:T(8,128)(2,1)}, u32[]{:S(2)}) copy-start(bf16[128,512]{1,0:T(8,128)(2,1)} %refs_1_.1) | copy-start | bytes 393220
  4.0 0.9 %copy-start.3 = (bf16[128,512]{1,0:T(8,128)(2,1)S(1)}, bf16[128,512]{1,0:T(8,128)(2,1)}, u32[]{:S(2)}) copy-start(bf16[128,512]{1,0:T(8,128)(2,1)} %refs_2_.1) | copy-start | bytes 393220
  4.9 0.9 %copy-start.4 = (bf16[128,512]{1,0:T(8,128)(2,1)S(1)}, bf16[128,512]{1,0:T(8,128)(2,1)}, u32[]{:S(2)}) copy-start(bf16[128,512]{1,0:T(8,128)(2,1)} %refs_3_.1) | copy-start | bytes 393220
  5.8 0.9 %copy-start.5 = (bf16[128,512]{1,0:T(8,128)(2,1)S(1)}, bf16[128,512]{1,0:T(8,128)(2,1)}, u32[]{:S(2)}) copy-start(bf16[128,512]{1,0:T(8,128)(2,1)} %refs_4_.1) | copy-start | bytes 393220
  6.8 0.9 %copy-start.6 = (bf16[128,512]{1,0:T(8,128)(2,1)S(1)}, bf16[128,512]{1,0:T(8,128)(2,1)}, u32[]{:S(2)}) copy-start(bf16[128,512]{1,0:T(8,128)(2,1)} %refs_6_.1) | copy-start | bytes 393220

commit v3 on v2

--- a/solution.py
+++ b/solution.py
@@ -31,19 +31,9 @@
     return lax.broadcasted_iota(jnp.int32, shape, dim)
 
 
-def local_kernel(
-    len_ref, *refs,
-):
-    sources, (rows_ref, maps_ref, xy_ref, w_ref, vg_ref) = refs[:7], refs[7:12]
-    staged, sems = refs[12:19], refs[19]
-    copies = [
-        pltpu.make_async_copy(src, dst, sems.at[i]) for i, (src, dst) in enumerate(zip(sources, staged))
-    ]
-    for copy in copies:
-        copy.start()
-    for copy in copies:
-        copy.wait()
-    r_ref, k_ref, v_ref, kap_ref, rem_ref, rate_ref, g_ref = staged
+def local_kernel(len_ref, *refs):
+    r_ref, k_ref, v_ref, kap_ref, rem_ref, rate_ref, g_ref = [refs[0].at[i] for i in range(7)]
+    rows_ref, maps_ref, xy_ref, w_ref, vg_ref = refs[1:]
     T, C = r_ref.shape
     live = (iota((T, 1), 0) < len_ref[0]).astype(F32)
     left = iota((T, 2 * HS), 1) < HS
@@ -68,6 +58,9 @@
     rows_ref[4] = k
     rows_ref[5] = v
     rows_ref[6] = g
+    last = iota((T, 1), 0) == T - 1
+    rows_ref[7] = pltpu.roll(kap, T - 1, 0)
+    rows_ref[8] = jnp.where(last, 1.0, pltpu.roll(jnp.exp(-rate), T - 1, 0))
     tril = (iota((T, T), 0) >= iota((T, T), 1)).astype(F32)
     cs = lax.dot_general(tril, rate, NN, precision=lax.Precision.HIGHEST, preferred_element_type=F32)
     mid = cs[T // 2 - 1:T // 2, :]
@@ -227,26 +220,35 @@
 ):
     T, C = gr_ref.shape
     pairs = C // 128
-    lane_left = iota((HS, 128), 1) < HS
-
-    def pack(which, p, a, b):
-        packs[which, 0, p] = jnp.where(lane_left, a, pltpu.roll(b, HS, 1))
-        packs[which, 1, p] = jnp.where(lane_left, pltpu.roll(a, HS, 1), b)
+    after = iota((HS, T), 1) < T - 1
+    src, dst = iota((2 * T, 2 * T), 0), iota((2 * T, 2 * T), 1)
+    moved = (src % T) // 8 * 16 + src // T * 8 + src % 8
+    order = (moved == dst).astype(BF16)
+
+    def arrange(way, p, factor, exact):
+        high, rest = halves(factor)
+        terms = [
+            lax.dot_general(m, order, NN, preferred_element_type=F32).astype(BF16)
+            for m in (high, rest, exact.astype(BF16))
+        ]
+        for quarter in range(T // 32):
+            cols = slice(quarter * HS, (quarter + 1) * HS)
+            parts = [terms[i][:, cols] for i in (0, 1, 0, 2)]
+            packs[way, quarter, p] = jnp.concatenate(parts, axis=1)
 
     for p in range(pairs):
         ha, hb = 2 * p, 2 * p + 1
         state, adjoint = carry_ref[p, 0], carry_ref[p, 1]
         cut = lambda a: (a[:, :HS], a[:, HS:])
+        side = lambda a: jnp.concatenate(a, axis=1)
         along = [dot3(s, xy_ref[h, :HS]) + xy_ref[h, HS:] for s, h in zip(cut(state), (ha, hb))]
         beta = [dot3(s, w_ref[h, :HS]) + w_ref[h, HS:] for s, h in zip(cut(adjoint), (ha, hb))]
-        pack(0, p, *along)
-        pack(1, p, *beta)
-        pack(2, p, *[vg_ref[0, h * HS:(h + 1) * HS, :] for h in (ha, hb)])
-        pack(3, p, *[vg_ref[1, h * HS:(h + 1) * HS, :] for h in (ha, hb)])
+        beta = [jnp.where(after, pltpu.roll(m, T - 1, 1), 0.0) for m in beta]
+        arrange(0, p, side(along), side([vg_ref[0, h * HS:(h + 1) * HS, :] for h in (ha, hb)]))
+        arrange(1, p, side(beta), side([vg_ref[1, h * HS:(h + 1) * HS, :] for h in (ha, hb)]))
         st[p] = state
         lt[p] = adjoint
 
-    offset = jnp.where(lane_left, 0, HS)
     head_mask = (iota((8, C), 0) == iota((8, C), 1) // HS).astype(F32)
     own = iota((32, 256), 0) // 8 == iota((32, 256), 1) // HS
 
@@ -280,38 +282,49 @@
         out_k[pl.ds(base, 8), :] = jnp.concatenate(sums_k, axis=0)
         out_v[pl.ds(base, 8), :] = jnp.concatenate(sums_v, axis=0)
 
-    def step(group, _):
-        base = pl.multiple_of(group * 8, 8)
-        base_b = pl.multiple_of(T - 8 - base, 8)
-        half = base // HS
-        half_b = base_b // HS
-        at = offset + (base - half * HS)
-        at_b = offset + (base_b - half_b * HS)
-        spread = lambda a, i: jnp.take_along_axis(a, i, axis=1)
-        for p in range(pairs):
-            cols = slice(p * 128, (p + 1) * 128)
-            rows = [rows_ref[n, pl.ds(base, 8), cols] for n in (0, 2, 4)]
-            along, vals = packs[0, half, p], packs[2, half, p]
-            s = st[p]
-            for j in range(8):
-                d, e, k = [a[j:j + 1, :] for a in rows]
-                s = s * d - spread(along, at + j) * e + spread(vals, at + j) * k
-                lowf[j * HS:(j + 1) * HS, cols] = s.astype(BF16)
-            st[p] = s
-            rows = [rows_ref[n, pl.ds(base_b, 8), cols] for n in (0, 1, 3)]
-            beta, grads = packs[1, half_b, p], packs[3, half_b, p]
-            c = lt[p]
-            for j in reversed(range(8)):
-                d, u, r = [a[j:j + 1, :] for a in rows]
-                adj = c + spread(grads, at_b + j) * r
-                lowb[j * HS:(j + 1) * HS, cols] = adj.astype(BF16)
-                c = adj * d - spread(beta, at_b + j) * u
-            lt[p] = c
-        contract(base, lowf, 3, 6, mix_acc, gr_acc)
-        contract(base_b, lowb, 4, 5, gv_acc, gk_acc)
+    r16, l16 = iota((16, 128), 0), iota((16, 128), 1)
+    picks = [(r16 // 8 == l16 // HS) & (r16 % 8 == j) for j in range(8)]
+    none = jnp.zeros((16, 128), BF16)
+
+    def fresh(way, quarter, octet, p, factors, exacts):
+        columns = []
+        for j in range(8):
+            high, rest = halves(jnp.where(picks[j], -factors[j:j + 1, :], 0.0))
+            exact = jnp.where(picks[j], exacts[j:j + 1, :], 0.0).astype(BF16)
+            blocks = []
+            for term in (high, high, rest, exact):
+                blocks += [term if at == octet else none for at in range(4)]
+            columns.append(jnp.concatenate(blocks, axis=0))
+        weights = jnp.concatenate(columns, axis=1)
+        return lax.dot_general(packs[way, quarter, p], weights, NN, preferred_element_type=F32)
+
+    def quarters(quarter, _):
+        quarter_b = T // 32 - 1 - quarter
+        for octet in range(4):
+            octet_b = 3 - octet
+            base = pl.multiple_of(quarter * 32 + octet * 8, 8)
+            base_b = pl.multiple_of(quarter_b * 32 + octet_b * 8, 8)
+            for p in range(pairs):
+                cols = slice(p * 128, (p + 1) * 128)
+                d, e, k = [rows_ref[n, pl.ds(base, 8), cols] for n in (0, 2, 4)]
+                new = fresh(0, quarter, octet, p, e, k)
+                s = st[p]
+                for j in range(8):
+                    s = s * d[j:j + 1, :] + new[:, j * 128:(j + 1) * 128]
+                    lowf[j * HS:(j + 1) * HS, cols] = s.astype(BF16)
+                st[p] = s
+                d, u, r = [rows_ref[n, pl.ds(base_b, 8), cols] for n in (8, 7, 3)]
+                new = fresh(1, quarter_b, octet_b, p, u, r)
+                c = lt[p]
+                for j in reversed(range(8)):
+                    c = c * d[j:j + 1, :] + new[:, j * 128:(j + 1) * 128]
+                    lowb[j * HS:(j + 1) * HS, cols] = c.astype(BF16)
+                lt[p] = c
+            contract(base, lowf, 3, 6, mix_acc, gr_acc)
+            contract(base_b, lowb, 4, 5, gv_acc, gk_acc)
         return 0
 
-    lax.fori_loop(0, T // 8, step, 0)
+    lax.fori_loop(0, T // 32, quarters, 0)
     gr_ref[...] = gr_acc[...].astype(BF16)
     gk_ref[...] = gk_acc[...].astype(BF16)
     mix_ref[...] = mix_acc[...].astype(BF16)
@@ -326,20 +339,23 @@
     sds = jax.ShapeDtypeStruct
     pairs = heads // 2
     arrays = (receptance, token_key, token_value, kappa_raw, removal, decay_rate, grad_output)
+    which = lax.broadcasted_iota(jnp.int32, (len(arrays), T, C), 0)
+    together = jnp.zeros((len(arrays), T, C), F32)
+    for i, a in enumerate(arrays):
+        together = jnp.where(which == i, a.astype(F32)[None], together)
     rows, maps, xy, w, vg = pl.pallas_call(
         local_kernel,
         out_shape=(
-            sds((7, T, C), F32),
+            sds((9, T, C), F32),
             sds((pairs, 3, HS, 2 * HS), F32),
             sds((heads, 2 * HS, T), F32),
             sds((heads, 2 * HS, T), F32),
             sds((2, C, T), F32),
         ),
-        in_specs=[smem] + [pl.BlockSpec(memory_space=pltpu.MemorySpace.HBM)] * 7,
+        in_specs=[smem, vmem],
         out_specs=(vmem,) * 5,
-        scratch_shapes=[pltpu.VMEM((T, C), a.dtype) for a in arrays] + [pltpu.SemaphoreType.DMA((7,))],
         compiler_params=pltpu.CompilerParams(vmem_limit_bytes=32 * 1024 * 1024),
-    )(shard_length, *arrays)
+    )(shard_length, together)
     count = lax.axis_size("ctx")
     groups = count // pairs
     dma = pltpu.SemaphoreType.DMA
@@ -370,7 +386,7 @@
         scratch_shapes=[
             pltpu.VMEM((pairs, HS, 2 * HS), F32),
             pltpu.VMEM((pairs, HS, 2 * HS), F32),
-            pltpu.VMEM((4, 2, pairs, HS, 2 * HS), F32),
+            pltpu.VMEM((2, T // 32, pairs, HS, 4 * HS), BF16),
             pltpu.VMEM((8 * HS, C), BF16),
             pltpu.VMEM((8 * HS, C), BF16),
         ] + [pltpu.VMEM((T, C), F32)] * 4,

time: 73.1 us -> 61.6 us (0.84)
  Pallas kernels: 65.2 us -> 54 us
  local copies, waits for them, and re-layouts: 6.37 us -> 0.01 us
  other arithmetic: 0 us -> 5.83 us
    pallas_call x1, Pallas kernels: 31.8 us -> 21.5 us  [local(): pl.pallas_call(exact_kernel, out_shape=(sds((T, C), BF16),) * 4, in_specs...]
    unnamed x14 -> x4, local copies, waits for them, and re-layouts: 6.37 us -> 0.01 us
    convert_element_type x0 -> x6, other arithmetic: none -> 4.65 us  [local(): together = jnp.where(which == i, a.astype(F32)[None], together)]
    select_n x0 -> x1, other arithmetic: none -> 1.16 us  [local(): together = jnp.where(which == i, a.astype(F32)[None], together)]
    pallas_call x1, Pallas kernels: 11.1 us -> 10.1 us  [local(): pl.pallas_call(local_kernel, out_shape=(sds((9, T, C), F32), sds((pairs,...]
where the time goes in v3:
time: 61.6 us; the launch traced here: 61.3 us
  Pallas kernels  54 us (88%)
  other arithmetic  5.83 us (9%)
  between operations  1.45 us (2%)
    pallas_call x1, Pallas kernels, local(): pl.pallas_call(functools.partial(carry_kernel, count), out_shape=sds((pai...  22.4 us
    pallas_call x1, Pallas kernels, local(): pl.pallas_call(exact_kernel, out_shape=(sds((T, C), BF16),) * 4, in_specs...  21.5 us
    pallas_call x1, Pallas kernels, local(): pl.pallas_call(local_kernel, out_shape=(sds((9, T, C), F32), sds((pairs,...  10.1 us
    convert_element_type x6, other arithmetic, local(): together = jnp.where(which == i, a.astype(F32)[None], together)  4.65 us

profile of v3, /device:TPU:1, one launch (start us, length us, event | category | flops | bytes accessed | tf_op | source)
XLA Modules:
  0.0 61.3 jit_solution(8167992576931756062)
XLA Ops:
  0.6 0.0 copy-start.1
  0.6 0.0 copy-start
  1.4 0.9 %convert_element_type.23 = f32[128,512]{1,0:T(8,128)S(1)} convert(bf16[128,512]{1,0:T(8,128)(2,1)} %param.8) | non-fusion elementwise | flops 65536 | bytes 393216 | tf_op jit(solution)/shard_map/convert_element_type | solution.py:345
  2.3 0.9 %convert_element_type.22 = f32[128,512]{1,0:T(8,128)S(1)} convert(bf16[128,512]{1,0:T(8,128)(2,1)} %param.9) | non-fusion elementwise | flops 65536 | bytes 393216 | tf_op jit(solution)/shard_map/convert_element_type | solution.py:345
  3.3 0.9 %convert_element_type.21 = f32[128,512]{1,0:T(8,128)S(1)} convert(bf16[128,512]{1,0:T(8,128)(2,1)} %param.10) | non-fusion elementwise | flops 65536 | bytes 393216 | tf_op jit(solution)/shard_map/convert_element_type | solution.py:345
  4.2 0.9 %convert_element_type.20 = f32[128,512]{1,0:T(8,128)S(1)} convert(bf16[128,512]{1,0:T(8,128)(2,1)} %param.11) | non-fusion elementwise | flops 65536 | bytes 393216 | tf_op jit(solution)/shard_map/convert_element_type | solution.py:345
  5.1 0.9 %convert_element_type.19 = f32[128,512]{1,0:T(8,128)S(1)} convert(bf16[128,512]{1,0:T(8,128)(2,1)} %param.12) | non-fusion elementwise | flops 65536 | bytes 393216 | tf_op jit(solution)/shard_map/convert_element_type | solution.py:345
  6.1 0.0 copy-done.1
  6.1 0.0 copy-done
  6.1 1.2 %select_select_fusion.refs_0_ = f32[7,128,512]{2,1,0:T(8,128)S(1)} fusion(f32[128,512]{1,0:T(8,128)S(1)} %convert_element_type.23, f32[128,512]{1,0:T(8,128)S(1)} %convert_element_type.22, f32[128,512]{1,0:T(8,128)S(1)} %convert_element_type.21, f32[128,512]{1,0:T(8,128)S(1)} %convert_element_type.20, f32[128,512]{1,0:T(8,128)S(1)} %convert_element_type.19, ...), kind=kLoop, calls=%fused_computation | loop fusion | flops 3211264 | bytes 3670065 | tf_op jit(solution)/shard_map/jit(_where)/select_n | solution.py:345
  7.3 10.1 %shard_map.111 = (f32[9,128,512]{2,1,0:T(8,128)S(1)}, f32[4,3,64,128]{3,2,1,0:T(8,128)S(1)}, f32[8,128,128]{2,1,0:T(8,128)S(1)}, f32[8,128,128]{2,1,0:T(8,128)S(1)}, f32[2,512,128]{2,1,0:T(8,128)S(1)}) custom-call(s32[1]{0:T(128)S(6)} %copy.12.len_ref, f32[7,128,512]{2,1,0:T(8,128)S(1)} %select_select_fusion.refs_0_), custom_call_target="tpu_custom_call" | custom-call | tf_op jit(solution)/shard_map/pallas_call | solution.py:346
  17.4 22.4 %shard_map.112.carry_ref = f32[4,2,64,128]{3,2,1,0:T(8,128)S(1)} custom-call(f32[4,3,64,128]{3,2,1,0:T(8,128)S(1)} %get-tuple-element.9.maps_ref), custom_call_target="tpu_custom_call" | custom-call | tf_op jit(solution)/shard_map/pallas_call | solution.py:362
  39.9 21.5 %shard_map.113 = (bf16[128,512]{1,0:T(8,128)(2,1)}, bf16[128,512]{1,0:T(8,128)(2,1)}, bf16[128,512]{1,0:T(8,128)(2,1)}, bf16[128,512]{1,0:T(8,128)(2,1)}) custom-call(f32[4,2,64,128]{3,2,1,0:T(8,128)S(1)} %shard_map.112.carry_ref, f32[9,128,512]{2,1,0:T(8,128)S(1)} %get-tuple-element.10.rows_ref, f32[8,128,128]{2,1,0:T(8,128)S(1)} %get-tuple-element.11.xy_ref, ...), custom_call_target="tpu_custom_call" | custom-call | tf_op jit(solution)/shard_map/pallas_call | solution.py:381
  (5 shorter events, 0.0 us)
Async XLA Ops:
  0.6 5.4 %copy-start.1 = (bf16[128,512]{1,0:T(8,128)(2,1)S(1)}, bf16[128,512]{1,0:T(8,128)(2,1)}, u32[]{:S(2)}) copy-start(bf16[128,512]{1,0:T(8,128)(2,1)} %param.15) | copy-start | bytes 393220
  0.6 5.5 %copy-start = (f32[128,512]{1,0:T(8,128)S(1)}, f32[128,512]{1,0:T(8,128)}, u32[]{:S(2)}) copy-start(f32[128,512]{1,0:T(8,128)} %param.13) | copy-start | bytes 786436

commit v4 on v3

--- a/solution.py
+++ b/solution.py
@@ -32,8 +32,9 @@
 
 
 def local_kernel(len_ref, *refs):
-    r_ref, k_ref, v_ref, kap_ref, rem_ref, rate_ref, g_ref = [refs[0].at[i] for i in range(7)]
-    rows_ref, maps_ref, xy_ref, w_ref, vg_ref = refs[1:]
+    r_ref, k_ref, v_ref, kap_ref, rem_ref, g_ref = [refs[0].at[i] for i in range(6)]
+    rate_ref = refs[1]
+    rows_ref, maps_ref, xy_ref, w_ref, vg_ref = refs[2:]
     T, C = r_ref.shape
     live = (iota((T, 1), 0) < len_ref[0]).astype(F32)
     left = iota((T, 2 * HS), 1) < HS
@@ -338,11 +339,11 @@
     smem = pl.BlockSpec(memory_space=pltpu.SMEM)
     sds = jax.ShapeDtypeStruct
     pairs = heads // 2
-    arrays = (receptance, token_key, token_value, kappa_raw, removal, decay_rate, grad_output)
+    arrays = (receptance, token_key, token_value, kappa_raw, removal, grad_output)
     which = lax.broadcasted_iota(jnp.int32, (len(arrays), T, C), 0)
-    together = jnp.zeros((len(arrays), T, C), F32)
+    together = jnp.zeros((len(arrays), T, C), BF16)
     for i, a in enumerate(arrays):
-        together = jnp.where(which == i, a.astype(F32)[None], together)
+        together = jnp.where(which == i, a[None], together)
     rows, maps, xy, w, vg = pl.pallas_call(
         local_kernel,
         out_shape=(
@@ -352,10 +353,10 @@
             sds((heads, 2 * HS, T), F32),
             sds((2, C, T), F32),
         ),
-        in_specs=[smem, vmem],
+        in_specs=[smem, vmem, vmem],
         out_specs=(vmem,) * 5,
         compiler_params=pltpu.CompilerParams(vmem_limit_bytes=32 * 1024 * 1024),
-    )(shard_length, together)
+    )(shard_length, together, decay_rate)
     count = lax.axis_size("ctx")
     groups = count // pairs
     dma = pltpu.SemaphoreType.DMA

time: 61.6 us -> 58 us (0.942)
  other arithmetic: 5.83 us -> 1.56 us
  local copies, waits for them, and re-layouts: 0.01 us -> 0.95 us
    convert_element_type x6 -> x0, other arithmetic: 4.65 us -> none  [local(): together = jnp.where(which == i, a.astype(F32)[None], together)]
    unnamed x4 -> x2, local copies, waits for them, and re-layouts: 0.01 us -> 0.95 us
where the time goes in v4:
time: 58 us; the launch traced here: 57.8 us
  Pallas kernels  54 us (93%)
  other arithmetic  1.56 us (3%)
  between operations  1.33 us (2%)
  local copies, waits for them, and re-layouts  0.95 us (2%)
    pallas_call x1, Pallas kernels, local(): pl.pallas_call(functools.partial(carry_kernel, count), out_shape=sds((pai...  22.4 us
    pallas_call x1, Pallas kernels, local(): pl.pallas_call(exact_kernel, out_shape=(sds((T, C), BF16),) * 4, in_specs...  21.5 us
    pallas_call x1, Pallas kernels, local(): pl.pallas_call(local_kernel, out_shape=(sds((9, T, C), F32), sds((pairs,...  10.1 us
    select_n x1, other arithmetic, local(): together = jnp.where(which == i, a[None], together)  1.55 us

profile of v4, /device:TPU:1, one launch (start us, length us, event | category | flops | bytes accessed | tf_op | source)
XLA Modules:
  0.0 57.8 jit_solution(18324280756995293858)
XLA Ops:
  1.3 1.5 %select_select_fusion.refs_0_ = bf16[6,128,512]{2,1,0:T(8,128)(2,1)S(1)} fusion(pred[6]{0:T(512)(128)(4,1)S(1)} %get-tuple-element.14, pred[6]{0:T(512)(128)(4,1)S(1)} %get-tuple-element.15, pred[6]{0:T(512)(128)(4,1)S(1)} %get-tuple-element.16, pred[6]{0:T(512)(128)(4,1)S(1)} %get-tuple-element.17, pred[6]{0:T(512)(128)(4,1)S(1)} %get-tuple-element.18, ...), kind=kLoop, calls=%fused_computation | loop fusion | flops 2359296 | bytes 1572900 | tf_op jit(solution)/shard_map/jit(_where)/select_n | solution.py:346
  2.9 0.0 copy-start
  2.9 0.9 %copy-done = f32[128,512]{1,0:T(8,128)S(1)} copy-done((f32[128,512]{1,0:T(8,128)S(1)}, f32[128,512]{1,0:T(8,128)}, u32[]{:S(2)}) %copy-start) | copy-done | bytes 262168
  3.8 10.1 %shard_map.111 = (f32[9,128,512]{2,1,0:T(8,128)S(1)}, f32[4,3,64,128]{3,2,1,0:T(8,128)S(1)}, f32[8,128,128]{2,1,0:T(8,128)S(1)}, f32[8,128,128]{2,1,0:T(8,128)S(1)}, f32[2,512,128]{2,1,0:T(8,128)S(1)}) custom-call(s32[1]{0:T(128)S(6)} %copy.12.len_ref, bf16[6,128,512]{2,1,0:T(8,128)(2,1)S(1)} %select_select_fusion.refs_0_, f32[128,512]{1,0:T(8,128)S(1)} %copy-done), custom_call_target="tpu_custom_call" | custom-call | tf_op jit(solution)/shard_map/pallas_call | solution.py:347
  13.9 22.4 %shard_map.112.carry_ref = f32[4,2,64,128]{3,2,1,0:T(8,128)S(1)} custom-call(f32[4,3,64,128]{3,2,1,0:T(8,128)S(1)} %get-tuple-element.9.maps_ref), custom_call_target="tpu_custom_call" | custom-call | tf_op jit(solution)/shard_map/pallas_call | solution.py:363
  36.4 21.5 %shard_map.113 = (bf16[128,512]{1,0:T(8,128)(2,1)}, bf16[128,512]{1,0:T(8,128)(2,1)}, bf16[128,512]{1,0:T(8,128)(2,1)}, bf16[128,512]{1,0:T(8,128)(2,1)}) custom-call(f32[4,2,64,128]{3,2,1,0:T(8,128)S(1)} %shard_map.112.carry_ref, f32[9,128,512]{2,1,0:T(8,128)S(1)} %get-tuple-element.10.rows_ref, f32[8,128,128]{2,1,0:T(8,128)S(1)} %get-tuple-element.11.xy_ref, ...), custom_call_target="tpu_custom_call" | custom-call | tf_op jit(solution)/shard_map/pallas_call | solution.py:382
  (3 shorter events, 0.0 us)
Async XLA Ops:
  2.9 1.0 %copy-start = (f32[128,512]{1,0:T(8,128)S(1)}, f32[128,512]{1,0:T(8,128)}, u32[]{:S(2)}) copy-start(f32[128,512]{1,0:T(8,128)} %refs_1_.1) | copy-start | bytes 786436
